TPU v7x, 256 devices: a whole 4x4x8 slice. The times are simulated.
256 devices in a mesh: blk: 16 (over y_hi, z), mer: 8 (over x, core), ply: 2 (over y_lo).
Axes of the slice: x: 4, y: 4 (y_hi: 2, y_lo: 2; y = y_hi * 2 + y_lo), z: 8, core: 2. Of those that a mesh axis runs over, the one named last changes fastest.
Arguments:
- loads: float32 [16, 8, 1536, 128], P('blk', 'mer', 'ply'), may hold values from -6 to 6
- schur: float32 [16, 8, 1536, 1536], P('blk', 'mer', 'ply'), as said below
- local_inverse: float32 [16, 8, 1536, 1536], P('blk', 'mer', 'ply'), as said below
- psi: float32 [16, 8, 1536, 8], P('blk', 'mer', 'ply'), may hold values from -0.21875 to 0.21875
- face_map: int32 [16, 8, 2, 4, 192], P('blk', 'mer', 'ply'), may hold values from 0 to 191, as said below
- primal_list: int32 [16, 8, 2, 8], P('blk', 'mer', 'ply'), may hold values from 0 to 2047, as said below
- coarse_inverse: float32 [2048, 2048], P(('blk', 'mer', 'ply')), as said below
Outputs:
- solution: float32 [16, 8, 1536, 128], P('blk', 'mer', 'ply')
- residual: float32 [16, 8, 1536, 128], P('blk', 'mer', 'ply')
Inputs may be any that keep to these rules, and one draw needn't show every extreme that they name: schur is symmetric and positive definite for every substructure. local_inverse is symmetric and positive definite for every substructure. coarse_inverse is symmetric and positive definite. Each face_map[b, m, p, f] is a permutation of 0 to 191; face_map[b, m, p, 0] is the inverse permutation of face_map[b - 1, m, p, 1] (cycle index modulo 16), and face_map[b, m, p, 2] is the inverse of face_map[b, m - 1, p, 3] for m > 0. `primal_list`: coarse unknown o of ply group (b, m, p) is ((b * 8 + m) * 2 + p) * 8 + o; every slot names a coarse unknown of its own ply group or of the ply group with the same m and p at cycle index b - 1 or b + 1 (modulo 16), or with the same b and p at meridian index m - 1 or m + 1.
All inputs are finite; a program needn't handle non-finite values.
Results may differ from a plain program's by a relative error of at most 0.0003.
Values sent between devices are 32-bit elements; how exact they have to be, the bound alone decides.
A program may use at most 64 MiB of HBM per device.

v0:
```python
import jax
import jax.numpy as jnp
from jax import lax
from jax.sharding import PartitionSpec as P

ITERS = 4


HIGH = lax.Precision.HIGHEST


def padded(block, sides, width, periodic):
    for axis, dim in sides:
        count = lax.axis_size(axis)
        forward = [(i, i + 1) for i in range(count - 1)]
        if periodic:
            forward.append((count - 1, 0))
        backward = [(target, source) for source, target in forward]
        low = lax.ppermute(
            lax.slice_in_dim(block, block.shape[dim] - width, None, axis=dim), axis, forward
        )
        high = lax.ppermute(lax.slice_in_dim(block, 0, width, axis=dim), axis, backward)
        block = jnp.concatenate([low, block, high], axis=dim)
    return block


def local(loads, schur, local_inverse, psi, face_map, primal_list, coarse_inverse):
    force = loads[0, 0]
    stiffness = schur[0, 0]
    neumann = local_inverse[0, 0]
    basis = psi[0, 0]
    links = face_map[0, 0, 0]
    slots = primal_list[0, 0, 0]
    half, cases = force.shape
    face = half // 4
    owned = coarse_inverse.shape[0]
    cycle_pos = lax.axis_index("blk")
    cycle_count = lax.axis_size("blk")
    mer_pos = lax.axis_index("mer")
    mer_count = lax.axis_size("mer")
    ply_pos = lax.axis_index("ply")
    ply_count = lax.axis_size("ply")
    lo_end = jnp.where(mer_pos == 0, 1.0, 0.5).astype(jnp.float32)
    hi_end = jnp.where(mer_pos == mer_count - 1, 1.0, 0.5).astype(jnp.float32)
    per_face = jnp.stack([jnp.float32(0.5), jnp.float32(0.5), lo_end, hi_end])
    weights = jnp.repeat(per_face, face)[:, None]
    self_id = (cycle_pos * mer_count + mer_pos) * ply_count + ply_pos
    cycle_prev = ((cycle_pos - 1) % cycle_count * mer_count + mer_pos) * ply_count + ply_pos
    cycle_next = ((cycle_pos + 1) % cycle_count * mer_count + mer_pos) * ply_count + ply_pos
    mer_prev = jnp.where(mer_pos > 0, self_id - ply_count, -1)
    mer_next = jnp.where(mer_pos < mer_count - 1, self_id + ply_count, -1)
    targets = jnp.stack([self_id, cycle_prev, cycle_next, mer_prev, mer_next])
    owners = slots // owned
    offsets = slots % owned
    matches = owners[None, :] == targets[:, None]
    places = offsets[:, None] == jnp.arange(owned)[None, :]
    selector = (matches[:, :, None] & places[None, :, :]).astype(jnp.float32)

    def assemble(vec):
        faces = vec.reshape(4, face, cases)
        cycle = padded(faces[0:2], (("blk", 0),), 1, True)
        meridian = padded(faces[2:4], (("mer", 0),), 1, False)
        incoming = jnp.stack(
            [
                jnp.take(cycle[0], links[0], axis=0),
                jnp.take(cycle[3], links[1], axis=0),
                jnp.take(meridian[0], links[2], axis=0),
                jnp.take(meridian[3], links[3], axis=0),
            ]
        )
        return (faces + incoming).reshape(half, cases)

    def product(matrix, vec):
        return jnp.dot(
            matrix,
            lax.all_gather(vec, "ply", axis=0, tiled=True),
            precision=HIGH,
            preferred_element_type=jnp.float32,
        )

    def inner(left, right):
        return lax.psum(jnp.sum(weights * left * right, axis=0), ("blk", "mer", "ply"))

    def coarse_values(terms):
        total = coarse_inverse.shape[1]
        spots = (slots[:, None] == jnp.arange(total)[None, :]).astype(jnp.float32)
        spread = lax.dot_general(
            spots,
            terms,
            (((0,), (0,)), ((), ())),
            precision=HIGH,
            preferred_element_type=jnp.float32,
        )
        coarse_rhs = lax.psum(spread, ("blk", "mer", "ply"))
        owned_x = jnp.dot(
            coarse_inverse, coarse_rhs, precision=HIGH, preferred_element_type=jnp.float32
        )
        doubled = jnp.stack([owned_x, owned_x])
        cycle_out = padded(doubled, (("blk", 0),), 1, True)
        mer_out = padded(doubled, (("mer", 0),), 1, False)
        sources = jnp.stack([owned_x, cycle_out[0], cycle_out[3], mer_out[0], mer_out[3]])
        return jnp.einsum("tkc,tcr->kr", selector, sources, precision=HIGH)

    def precondition(residual):
        scaled = weights * residual
        local_part = product(neumann, scaled)
        terms = lax.dot_general(
            basis,
            scaled,
            (((0,), (0,)), ((), ())),
            precision=HIGH,
            preferred_element_type=jnp.float32,
        )
        picked = coarse_values(terms)
        correction = jnp.dot(basis, picked, precision=HIGH, preferred_element_type=jnp.float32)
        return assemble(weights * (local_part + correction))

    solution = jnp.zeros_like(force)
    residual = assemble(force)
    precond = precondition(residual)
    direction = precond
    rz = inner(residual, precond)
    for step in range(ITERS):
        image = assemble(product(stiffness, direction))
        alpha = rz / inner(direction, image)
        solution = solution + alpha * direction
        residual = residual - alpha * image
        if step + 1 < ITERS:
            precond = precondition(residual)
            rz_new = inner(residual, precond)
            direction = precond + rz_new / rz * direction
            rz = rz_new
    return (solution[None, None], residual[None, None])


def solution(mesh):
    in_specs = (
        P("blk", "mer", "ply", None),
        P("blk", "mer", "ply", None),
        P("blk", "mer", "ply", None),
        P("blk", "mer", "ply", None),
        P("blk", "mer", "ply", None, None),
        P("blk", "mer", "ply", None),
        P(("blk", "mer", "ply"), None),
    )
    out_specs = (P("blk", "mer", "ply", None), P("blk", "mer", "ply", None))
    return jax.shard_map(local, mesh=mesh, in_specs=in_specs, out_specs=out_specs, check_vma=False)
```

profile of v0, /device:TPU:1, one launch (start us, length us, event | category | flops | bytes accessed | tf_op | source)
XLA Modules:
  0.0 1865.0 jit_solution(471207286189628944)
XLA Ops:
  10.9 6.7 collective-permute-start.1
  31.9 9.8 all_gather.24
  41.7 241.8 %all-reduce.6.cloned.1.call-done = f32[2048,128]{1,0:T(8,128)} async-done(((f32[2048,128]{1,0:T(8,128)}), f32[2048,128]{1,0:T(8,128)}) %all-reduce.6.cloned.1.call-update) | async-done | bytes 1048592 | tf_op jit(solution)/shard_map/psum | solution.py:94
  286.8 7.2 fusion.14
  298.3 5.3 collective-permute-start.6
  322.0 10.0 all_gather.25
  332.0 7.3 fusion.16
  357.6 73.8 %all-reduce = (f32[128]{0:T(128)S(1)}, f32[128]{0:T(128)S(1)}) all-reduce(f32[128]{0:T(128)S(1)} %get-tuple-element.8, f32[128]{0:T(128)S(1)} %get-tuple-element.7), channel_id=1, replica_groups=mesh['blk'=16,'mer'=8,'ply'=2] {'blk','mer','ply'}, use_global_device_ids=true, to_apply=%region_2.4 | all-reduce | flops 256 | bytes 2048 | tf_op jit(solution)/shard_map/psum | solution.py:82
  433.8 10.8 all_gather.26
  444.7 237.8 %all-reduce.8.cloned.1.call-done = f32[2048,128]{1,0:T(8,128)} async-done(((f32[2048,128]{1,0:T(8,128)}), f32[2048,128]{1,0:T(8,128)}) %all-reduce.8.cloned.1.call-update) | async-done | bytes 1048592 | tf_op jit(solution)/shard_map/psum | solution.py:94
  685.9 7.2 fusion.12
  697.5 5.3 collective-permute-start.18
  721.1 74.3 %psum.88 = f32[128]{0:T(128)S(1)} all-reduce(f32[128]{0:T(128)S(1)} %get-tuple-element.23), channel_id=1, replica_groups=mesh['blk'=16,'mer'=8,'ply'=2] {'blk','mer','ply'}, use_global_device_ids=true, to_apply=%region_7.9 | all-reduce | flops 128 | bytes 1024 | tf_op jit(solution)/shard_map/psum | solution.py:82
  795.5 11.1 all_gather.27
  806.6 7.3 fusion.19
  831.2 73.3 %psum.89 = f32[128]{0:T(128)S(1)} all-reduce(f32[128]{0:T(128)S(1)} %get-tuple-element.21), channel_id=1, replica_groups=mesh['blk'=16,'mer'=8,'ply'=2] {'blk','mer','ply'}, use_global_device_ids=true, to_apply=%region_9.11 | all-reduce | flops 128 | bytes 1024 | tf_op jit(solution)/shard_map/psum | solution.py:82
  906.8 10.8 all_gather.28
  917.7 238.1 %all-reduce.10.cloned.1.call-done = f32[2048,128]{1,0:T(8,128)} async-done(((f32[2048,128]{1,0:T(8,128)}), f32[2048,128]{1,0:T(8,128)}) %all-reduce.10.cloned.1.call-update) | async-done | bytes 1048592 | tf_op jit(solution)/shard_map/psum | solution.py:94
  1159.1 7.3 fusion.10
  1170.7 5.3 collective-permute-start.30
  1195.2 74.3 %psum.91 = f32[128]{0:T(128)S(1)} all-reduce(f32[128]{0:T(128)S(1)} %get-tuple-element.19), channel_id=1, replica_groups=mesh['blk'=16,'mer'=8,'ply'=2] {'blk','mer','ply'}, use_global_device_ids=true, to_apply=%region_12.14 | all-reduce | flops 128 | bytes 1024 | tf_op jit(solution)/shard_map/psum | solution.py:82
  1269.6 10.9 all_gather.29
  1280.4 7.3 fusion.22
  1302.3 76.8 %psum.92 = f32[128]{0:T(128)S(1)} all-reduce(f32[128]{0:T(128)S(1)} %get-tuple-element.17), channel_id=1, replica_groups=mesh['blk'=16,'mer'=8,'ply'=2] {'blk','mer','ply'}, use_global_device_ids=true, to_apply=%region_14.16 | all-reduce | flops 128 | bytes 1024 | tf_op jit(solution)/shard_map/psum | solution.py:82
  1381.5 10.8 all_gather.30
  1392.4 238.3 %all-reduce.12.cloned.1.call-done = f32[2048,128]{1,0:T(8,128)} async-done(((f32[2048,128]{1,0:T(8,128)}), f32[2048,128]{1,0:T(8,128)}) %all-reduce.12.cloned.1.call-update) | async-done | bytes 1048592 | tf_op jit(solution)/shard_map/psum | solution.py:94
  1634.2 7.2 fusion.8
  1645.7 5.3 collective-permute-start.42
  1670.2 74.3 %psum.94 = f32[128]{0:T(128)S(1)} all-reduce(f32[128]{0:T(128)S(1)} %get-tuple-element.13), channel_id=1, replica_groups=mesh['blk'=16,'mer'=8,'ply'=2] {'blk','mer','ply'}, use_global_device_ids=true, to_apply=%region_17.19 | all-reduce | flops 128 | bytes 1024 | tf_op jit(solution)/shard_map/psum | solution.py:82
  1744.6 11.0 all_gather.31
  1755.6 7.3 fusion.25
  1781.7 73.2 %psum.95 = f32[128]{0:T(128)S(1)} all-reduce(f32[128]{0:T(128)S(1)} %get-tuple-element.11), channel_id=1, replica_groups=mesh['blk'=16,'mer'=8,'ply'=2] {'blk','mer','ply'}, use_global_device_ids=true, to_apply=%region_19.21 | all-reduce | flops 128 | bytes 1024 | tf_op jit(solution)/shard_map/psum | solution.py:82
  (327 shorter events, 202.1 us)
Async XLA Ops:
  7.2 276.3 %all-reduce.6.cloned.1.call-start = ((), (), s32[]{:S(2)}) async-start(), calls=%async_computation | async-start | bytes 2097152 | tf_op jit(solution)/shard_map/psum | solution.py:94
  8.4 17.2 collective-permute-start
  10.9 15.4 collective-permute-start.1
  17.6 9.4 collective-permute-start.2
  31.4 651.1 %all-reduce.8.cloned.1.call-start = ((), (), s32[]{:S(2)}) async-start(), calls=%async_computation.1 | async-start | bytes 2097152 | tf_op jit(solution)/shard_map/psum | solution.py:94
  285.4 20.1 %collective-permute-start.4 = (f32[1,8,128]{2,1,0:T(8,128)S(1)}, f32[1,8,128]{2,1,0:T(8,128)S(1)}, u32[]{:S(2)}, u32[]{:S(2)}) collective-permute-start(f32[1,8,128]{2,1,0:T(8,128)S(1)} %get-tuple-element.73), channel_id=1, source_target_pairs={{0,16},{16,32},{32,48},{48,64},{64,80},{80,96},{96,112},{112,128},... | collective-permute-start | bytes 12296 | tf_op jit(solution)/shard_map/ppermute | solution.py:19
  294.0 11.5 collective-permute-start.5
  311.8 8.2 collective-permute-start.8
  339.4 9.5 collective-permute-start.14
  347.0 8.4 collective-permute-start.12
  347.0 9.3 collective-permute-start.15
  433.8 722.0 %all-reduce.10.cloned.1.call-start = ((), (), s32[]{:S(2)}) async-start(), calls=%async_computation.2 | async-start | bytes 2097152 | tf_op jit(solution)/shard_map/psum | solution.py:94
  684.4 20.3 %collective-permute-start.16 = (f32[1,8,128]{2,1,0:T(8,128)S(1)}, f32[1,8,128]{2,1,0:T(8,128)S(1)}, u32[]{:S(2)}, u32[]{:S(2)}) collective-permute-start(f32[1,8,128]{2,1,0:T(8,128)S(1)} %get-tuple-element.75), channel_id=1, source_target_pairs={{0,16},{16,32},{32,48},{48,64},{64,80},{80,96},{96,112},{112,128},... | collective-permute-start | bytes 12296 | tf_op jit(solution)/shard_map/ppermute | solution.py:19
  693.2 11.5 collective-permute-start.17
  710.8 8.2 collective-permute-start.20
  814.0 8.0 collective-permute-start.26
  820.1 8.9 collective-permute-start.24
  820.1 9.8 collective-permute-start.27
  906.8 723.9 %all-reduce.12.cloned.1.call-start = ((), (), s32[]{:S(2)}) async-start(), calls=%async_computation.3 | async-start | bytes 2097152 | tf_op jit(solution)/shard_map/psum | solution.py:94
  1157.6 20.3 %collective-permute-start.28 = (f32[1,8,128]{2,1,0:T(8,128)S(1)}, f32[1,8,128]{2,1,0:T(8,128)S(1)}, u32[]{:S(2)}, u32[]{:S(2)}) collective-permute-start(f32[1,8,128]{2,1,0:T(8,128)S(1)} %get-tuple-element.77), channel_id=1, source_target_pairs={{0,16},{16,32},{32,48},{48,64},{64,80},{80,96},{96,112},{112,128},... | collective-permute-start | bytes 12296 | tf_op jit(solution)/shard_map/ppermute | solution.py:19
  1166.4 11.5 collective-permute-start.29
  1184.6 8.4 collective-permute-start.32
  1186.0 7.9 collective-permute-start.35
  1288.5 8.2 collective-permute-start.37
  1291.1 8.3 collective-permute-start.38
  1632.6 20.4 %collective-permute-start.40 = (f32[1,8,128]{2,1,0:T(8,128)S(1)}, f32[1,8,128]{2,1,0:T(8,128)S(1)}, u32[]{:S(2)}, u32[]{:S(2)}) collective-permute-start(f32[1,8,128]{2,1,0:T(8,128)S(1)} %get-tuple-element.79), channel_id=1, source_target_pairs={{0,16},{16,32},{32,48},{48,64},{64,80},{80,96},{96,112},{112,128},... | collective-permute-start | bytes 12296 | tf_op jit(solution)/shard_map/ppermute | solution.py:19
  1641.4 11.5 collective-permute-start.41
  1659.7 8.4 collective-permute-start.44
  1661.0 7.9 collective-permute-start.47
  1763.6 8.0 collective-permute-start.50
  1769.7 9.2 collective-permute-start.48
  1769.7 10.1 collective-permute-start.51
  (28 other events, 491.1 us)
Sparse Core Ops, SparseCore 0:
  31.5 251.9 all-reduce.5
  433.9 248.5 all-reduce.7
  906.9 248.7 all-reduce.9
  1381.7 248.9 all-reduce.11
where the time goes:
time: 1880 us; the launch traced here: 1860 us
  waiting for transfers between devices  994 us (53%)
  blocking collectives  605 us (32%)
  starting transfers between devices  127 us (7%)
  matrix products  77.9 us (4%)
  local copies, waits for them, and re-layouts  37.4 us (2%)
    psum x4, waiting for transfers between devices, coarse_values(): coarse_rhs = lax.psum(spread, ('blk', 'mer', 'ply'))  956 us
    psum x7, blocking collectives, inner(): lax.psum(jnp.sum(weights * left * right, axis=0), ('blk', 'mer', 'ply'))  520 us
    all_gather x8, blocking collectives, product(): lax.all_gather(vec, 'ply', axis=0, tiled=True)  85.2 us
    ppermute x26, starting transfers between devices, padded(): lax.ppermute(lax.slice_in_dim(block, 0, width, axis=dim), axis, backward)  64.1 us
    ppermute x26, starting transfers between devices, padded(): lax.ppermute(lax.slice_in_dim(block, block.shape[dim] - width, None, axis...  62.5 us
    dot_general x8, matrix products, product(): jnp.dot(matrix, lax.all_gather(vec, 'ply', axis=0, tiled=True), precision...  58 us
  transfers between devices with their start and end apart: 56, of which 19 were waited for; matrix products, arithmetic and copies ran while one was open for 3% of the time, Pallas kernels for 0%

commit v1 on v0

v1 whole, which is shorter than its diff:
```python
import functools

import jax
import jax.numpy as jnp
from jax import lax
from jax.experimental import pallas as pl
from jax.experimental.pallas import tpu as pltpu
from jax.sharding import PartitionSpec as P

ITERS = 4
EXCH = 2 * ITERS + 1
F32 = jnp.float32
BF16 = jnp.bfloat16
HIGH = lax.Precision.HIGHEST
MESH = pl.DeviceIdType.MESH
NT = (((1,), (1,)), ((), ()))


def halves(value):
    hi = value.astype(BF16)
    return hi, (value - hi.astype(F32)).astype(BF16)


def thirds(value):
    hi = value.astype(BF16)
    rest = value - hi.astype(F32)
    mid = rest.astype(BF16)
    return hi, mid, (rest - mid.astype(F32)).astype(BF16)


def dot(left, right):
    return jnp.dot(left, right, preferred_element_type=F32)


def remote(src, dst, send, recv, device):
    return pltpu.make_async_remote_copy(
        src_ref=src, dst_ref=dst, send_sem=send, recv_sem=recv, device_id=device, device_id_type=MESH
    )


def kernel(
    sizes,
    loads_ref, schur_ref, linv_ref, psi_ref, map_ref, list_ref, coarse_ref,
    x_ref, r_ref,
    lf, sf, lhi, llo, shi, slo,
    face_tx, face_rx, own, ply_rx,
    other, pdir, sraw, acc, gvec, tb, perm, psc, pst,
    nbr, dpad, wblk, cblk, lists,
    co1, ytx, co2, ar1, ar2, rz_ref,
    load_sem, face_ss, face_rs, ply_ss, ply_rs,
    nbr_ss, nbr_rs, win_ss, win_rs, list_ss, list_rs,
    co1_ss, co1_rs, co2_ss, co2_rs, ar1_ss, ar1_rs, ar2_ss, ar2_rs,
):
    nb, nm, npl = sizes
    ng = nm * npl
    half, cases = loads_ref.shape
    face = half // 4
    owned = coarse_ref.shape[0]
    b = lax.axis_index("blk")
    m = lax.axis_index("mer")
    p = lax.axis_index("ply")
    q = 1 - p
    mp = m * npl + p
    b_prev = lax.rem(b + nb - 1, nb)
    b_next = lax.rem(b + 1, nb)
    has_lo = m > 0
    has_hi = m < nm - 1
    weight = [
        0.5,
        0.5,
        jnp.where(has_lo, 0.5, 1.0).astype(F32),
        jnp.where(has_hi, 0.5, 1.0).astype(F32),
    ]
    partner = (b, m, q)
    neighbour = [(b_prev, m, p), (b_next, m, p), (b, m - 1, p), (b, m + 1, p)]
    exists = [None, None, has_lo, has_hi]

    def guarded(f, fn):
        if exists[f] is None:
            fn()
        else:
            pl.when(exists[f])(fn)

    def mp_device(index):
        return (b, lax.div(index, npl), lax.rem(index, npl))

    def blk_device(index):
        return (index, m, p)

    def spread(count, me, device_of, src_of, dst, send, recv):
        def step(j, carry):
            peer = lax.rem(me + j, count)
            remote(src_of(peer), dst, send, recv, device_of(peer)).start()
            return carry

        lax.fori_loop(1, count, step, 0)

    def fetch(index, source, side, target):
        column = pl.multiple_of(side * half, 128)
        return pltpu.make_async_copy(
            source.at[:, pl.ds(column, half)], target.at[index % 2], load_sem.at[index]
        )

    fetches = [
        fetch(0, linv_ref, p, lf),
        fetch(1, linv_ref, q, lf),
        fetch(2, schur_ref, p, sf),
        fetch(3, schur_ref, q, sf),
    ]
    for copy in fetches:
        copy.start()

    barrier = pltpu.get_barrier_semaphore()

    def greet(count, me, device_of):
        def step(j, carry):
            peer = lax.rem(me + j, count)
            pl.semaphore_signal(barrier, inc=1, device_id=device_of(peer), device_id_type=MESH)
            return carry

        lax.fori_loop(1, count, step, 0)

    greet(ng, mp, mp_device)
    greet(nb, b, blk_device)

    rows = lax.broadcasted_iota(jnp.int32, (face, face), 0)
    for f in range(4):
        perm[f] = jnp.where(rows == map_ref[f : f + 1, :], 1.0, 0.0).astype(BF16)

    for f in (2, 3):

        @pl.when(jnp.logical_not(exists[f]))
        def _():
            def clear(e, carry):
                face_rx[e, f] = jnp.zeros((face, cases), F32)
                return carry

            lax.fori_loop(0, EXCH, clear, 0)
            nbr[1 + f] = jnp.zeros(nbr.shape[1:], F32)

    lane = lax.broadcasted_iota(jnp.int32, (owned, lists.shape[2]), 1)
    sub = lax.broadcasted_iota(jnp.int32, (owned, lists.shape[2]), 0)
    mine = jnp.zeros_like(lane)
    for k in range(owned):
        mine = jnp.where(sub == k, list_ref[k], mine)
    lists[mp] = mine

    def permute(f, value):
        hi, mid, lo = thirds(value)
        out = dot(perm[f], jnp.concatenate([hi, mid, lo], axis=1))
        return (out[:, 2 * cases :] + out[:, cases : 2 * cases]) + out[:, :cases]

    def face_copy(e, f):
        return remote(
            face_tx.at[e, f], face_rx.at[e, f ^ 1], face_ss.at[e, f], face_rs.at[e, f ^ 1], neighbour[f]
        )

    def face_send(e, f, value):
        def go():
            face_tx[e, f] = permute(f, value)
            face_copy(e, f).start()

        guarded(f, go)

    def face_wait(e, f):
        guarded(
            f,
            lambda: remote(
                face_tx.at[e, f], face_rx.at[e, f], face_ss.at[e, f], face_rs.at[e, f], neighbour[f]
            ).wait_recv(),
        )

    def faces_sent(e):
        for f in range(4):
            guarded(f, lambda f=f: face_copy(e, f).wait_send())

    def ply_copy(e, pair):
        part = pl.ds(2 * pair, 2)
        return remote(own.at[e, part], ply_rx.at[e, part], ply_ss.at[e, pair], ply_rs.at[e, pair], partner)

    def batch(buffer, index, count, send, recv):
        block = buffer.at[index, pl.ds(0, count - 1)]
        return remote(block, block, send, recv, partner)

    def reduce_first(k, value):
        ar1[k, mp] = value
        spread(ng, mp, mp_device, lambda _: ar1.at[k, mp], ar1.at[k, mp], ar1_ss.at[k], ar1_rs.at[k])

    def reduce_second(k):
        batch(ar1, k, ng, ar1_ss.at[k], ar1_rs.at[k]).wait_recv()
        ar2[k, b] = jnp.sum(ar1[k], axis=0)
        spread(nb, b, blk_device, lambda _: ar2.at[k, b], ar2.at[k, b], ar2_ss.at[k], ar2_rs.at[k])

    def reduce_end(k):
        batch(ar2, k, nb, ar2_ss.at[k], ar2_rs.at[k]).wait_recv()
        return jnp.sum(ar2[k], axis=0)

    def reduce_sent(k):
        batch(ar1, k, ng, ar1_ss.at[k], ar1_rs.at[k]).wait_send()
        batch(ar2, k, nb, ar2_ss.at[k], ar2_rs.at[k]).wait_send()

    def store_split(side, f, value):
        hi, lo = halves(value)
        part = pl.ds(f * face, face)
        tb[side, part, pl.ds(0, cases)] = hi
        tb[side, part, pl.ds(cases, cases)] = lo

    def product(hi, lo, side):
        both = dot(hi[side], tb[side])
        small = dot(lo[side], tb[side, :, pl.ds(0, cases)])
        return (both[:, :cases] + both[:, cases:]) + small

    pl.semaphore_wait(barrier, ng - 1 + nb - 1)

    for f in (0, 1, 2, 3):
        face_send(0, f, loads_ref[pl.ds(f * face, face), :])

    slot_there = [2, 1, 4, 3]

    def nbr_copy(f):
        slot = slot_there[f]
        return remote(coarse_ref, nbr.at[slot], nbr_ss.at[f], nbr_rs.at[slot - 1], neighbour[f])

    for f in range(4):
        guarded(f, lambda f=f: nbr_copy(f).start())
    nbr[0] = coarse_ref[...]
    spread(ng, mp, mp_device, lambda _: lists.at[mp], lists.at[mp], list_ss.at[0], list_rs.at[0])

    psi = psi_ref[...]
    psi_hi, psi_lo = halves(psi)
    psi_hi = psi_hi.astype(F32)
    psc[...] = jnp.concatenate([psi_hi, psi_hi, psi_lo.astype(F32)], axis=1).astype(BF16)
    pick_r = lax.broadcasted_iota(jnp.int32, (2 * owned, 3 * owned), 0)
    pick_c = lax.broadcasted_iota(jnp.int32, (2 * owned, 3 * owned), 1)
    want = jnp.where(pick_r < owned, pick_r, pick_r + owned)
    pick = jnp.where(want == pick_c, 1.0, 0.0).astype(BF16)
    pst[...] = lax.dot_general(pick, psc[...], NT, preferred_element_type=F32).astype(BF16)

    def split_matrix(source, hi, lo):
        def step(i, carry):
            part = pl.ds(i * 64, 64)
            for side in range(2):
                a, c = halves(source[side, part, :])
                hi[side, part, :] = a
                lo[side, part, :] = c
            return carry

        lax.fori_loop(0, half // 64, step, 0)

    fetches[0].wait()
    fetches[1].wait()
    split_matrix(lf, lhi, llo)

    group = ng * owned
    this = (b * nm + m) * npl + p
    bases = [
        this * owned,
        ((b_prev * nm + m) * npl + p) * owned,
        ((b_next * nm + m) * npl + p) * owned,
        jnp.where(has_lo, (this - npl) * owned, -owned),
        jnp.where(has_hi, (this + npl) * owned, -owned),
    ]
    wide = lax.broadcasted_iota(jnp.int32, (owned, 5 * owned), 1)
    tall = lax.broadcasted_iota(jnp.int32, (owned, 5 * owned), 0)
    names = jnp.zeros_like(wide)
    for t in range(5):
        names = jnp.where(lax.div(wide, owned) == t, bases[t] + wide - t * owned, names)
    slots = jnp.zeros_like(wide)
    for k in range(owned):
        slots = jnp.where(tall == k, list_ref[k], slots)
    selector = jnp.where(slots == names, 1.0, 0.0).astype(F32)
    for f in range(4):
        guarded(
            f,
            lambda f=f: remote(
                coarse_ref, nbr.at[1 + f], nbr_ss.at[f], nbr_rs.at[f], neighbour[f]
            ).wait_recv(),
        )
    named = jnp.dot(
        selector, nbr[...].reshape(5 * owned, nbr.shape[2]), precision=HIGH, preferred_element_type=F32
    )
    for j in range(nb + 2):
        block = (j - 1) % nb
        dpad[j] = named[:, block * group : (block + 1) * group]
    wblk[b] = dpad[pl.ds(b, 3)]
    spread(nb, b, blk_device, lambda peer: dpad.at[pl.ds(peer, 3)], wblk.at[b], win_ss.at[0], win_rs.at[0])

    for f in (2, 3, 0, 1):
        face_wait(0, f)
        value = loads_ref[pl.ds(f * face, face), :] + face_rx[0, f]
        own[0, f] = value
        r_ref[pl.ds(f * face, face), :] = value
        other[f] = jnp.zeros((face, cases), F32)
        if f in (3, 1):
            ply_copy(0, f // 2).start()
    x_ref[...] = jnp.zeros_like(x_ref)
    pdir[...] = jnp.zeros_like(pdir)
    sraw[...] = jnp.zeros_like(sraw)
    rz_ref[...] = jnp.ones_like(rz_ref)

    block = lists.at[pl.ds(0, ng - 1)]
    remote(block, block, list_ss.at[0], list_rs.at[0], partner).wait_recv()
    names = lists[:, :, pl.ds(0, group)].reshape(group, group)
    column = lax.broadcasted_iota(jnp.int32, (group, group), 1)
    block = wblk.at[pl.ds(0, nb - 1)]
    remote(block, block, win_ss.at[0], win_rs.at[0], partner).wait_recv()
    total = jnp.zeros((nb * owned, group), F32)
    for j, start in enumerate((b_prev, b, b_next)):
        hot = jnp.where(names == column + start * group, 1.0, 0.0).astype(F32)
        window = wblk[:, j].reshape(nb * owned, group)
        total += lax.dot_general(window, hot, NT, precision=HIGH, preferred_element_type=F32)
    cblk[...] = total

    for f in range(4):
        guarded(f, lambda f=f: nbr_copy(f).wait_send())
    block = lists.at[pl.ds(0, ng - 1)]
    remote(block, block, list_ss.at[0], list_rs.at[0], partner).wait_send()
    block = wblk.at[pl.ds(0, nb - 1)]
    remote(block, block, win_ss.at[0], win_rs.at[0], partner).wait_send()
    faces_sent(0)

    def iteration(it, alpha):
        e1 = 1 + 2 * it
        e2 = 2 + 2 * it
        k1 = 2 * it
        k2 = 2 * it + 1

        for f in range(4):
            store_split(0, f, weight[f] * r_ref[pl.ds(f * face, face), :])
        parts = dot(pst[...], tb[0])
        terms = parts[:owned, :cases] + parts[:owned, cases:] + parts[owned:, :cases]
        co1[it, mp] = terms
        spread(ng, mp, mp_device, lambda _: co1.at[it, mp], co1.at[it, mp], co1_ss.at[it], co1_rs.at[it])
        acc[...] = product(lhi, llo, 0)

        batch(co1, it, ng, co1_ss.at[it], co1_rs.at[it]).wait_recv()
        y = jnp.dot(
            cblk[...], co1[it].reshape(group, cases), precision=HIGH, preferred_element_type=F32
        )
        ytx[it] = y.reshape(nb, owned, cases)
        spread(nb, b, blk_device, lambda peer: ytx.at[it, peer], co2.at[it, b], co2_ss.at[it], co2_rs.at[it])
        co2[it, b] = ytx[it, b]

        @pl.when(it == 0)
        def _():
            fetches[2].wait()
            fetches[3].wait()
            split_matrix(sf, shi, slo)

        for f in (2, 3, 0, 1):
            if f in (2, 0):
                ply_copy(e1 - 1, f // 2).wait_recv()
            value = other[f] + alpha * ply_rx[e1 - 1, f]
            other[f] = value
            store_split(1, f, weight[f] * value)
        acc[...] += product(lhi, llo, 1)

        batch(co2, it, nb, co2_ss.at[it], co2_rs.at[it]).wait_recv()
        picked = jnp.sum(co2[it], axis=0)
        pick_hi = picked.astype(BF16).astype(F32)
        stack = jnp.concatenate([pick_hi, picked - pick_hi, pick_hi], axis=0).astype(BF16)
        acc[...] += dot(psc[...], stack)

        partial = jnp.zeros((8, cases), F32)
        for f in (0, 1, 2, 3):
            part = pl.ds(f * face, face)
            value = weight[f] * acc[part, :]
            gvec[f] = value
            face_send(e1, f, value)
            partial += jnp.sum((value * r_ref[part, :]).reshape(face // 8, 8, cases), axis=0)
        reduce_first(k1, jnp.sum(partial, axis=0, keepdims=True))

        for f in (2, 3, 0, 1):
            face_wait(e1, f)
            value = gvec[f] + face_rx[e1, f]
            own[e1, f] = value
            if f in (3, 1):
                ply_copy(e1, f // 2).start()
            store_split(0, f, value)
        reduce_second(k1)

        acc[...] = product(shi, slo, 0)
        rz = reduce_end(k1)
        beta = jnp.where(it == 0, 0.0, rz / rz_ref[...])
        rz_ref[...] = rz
        for f in range(4):
            pdir[f] = own[e1, f] + beta * pdir[f]
        batch(co1, it, ng, co1_ss.at[it], co1_rs.at[it]).wait_send()
        batch(co2, it, nb, co2_ss.at[it], co2_rs.at[it]).wait_send()
        reduce_sent(k1)
        faces_sent(e1)
        for pair in range(2):
            ply_copy(e1 - 1, pair).wait_send()
        for f in (2, 3, 0, 1):
            if f in (2, 0):
                ply_copy(e1, f // 2).wait_recv()
            store_split(1, f, ply_rx[e1, f])
        acc[...] += product(shi, slo, 1)
        partial = jnp.zeros((8, cases), F32)
        for f in (0, 1, 2, 3):
            value = acc[pl.ds(f * face, face), :] + beta * sraw[f]
            sraw[f] = value
            face_send(e2, f, value)
            partial += jnp.sum((value * pdir[f]).reshape(face // 8, 8, cases), axis=0)
        reduce_first(k2, jnp.sum(partial, axis=0, keepdims=True))

        def assembled(f):
            face_wait(e2, f)
            own[e2, f] = sraw[f] + face_rx[e2, f]
            if f in (3, 1):

                @pl.when(it + 1 < ITERS)
                def _():
                    ply_copy(e2, f // 2).start()

        assembled(2)
        assembled(3)
        reduce_second(k2)
        assembled(0)
        assembled(1)
        for pair in range(2):
            ply_copy(e1, pair).wait_send()
        alpha = rz / reduce_end(k2)
        for f in range(4):
            part = pl.ds(f * face, face)
            x_ref[part, :] += alpha * pdir[f]
            r_ref[part, :] -= alpha * own[e2, f]
        reduce_sent(k2)
        faces_sent(e2)
        return -alpha

    lax.fori_loop(0, ITERS, iteration, jnp.ones((1, cases), F32))


def local(sizes, loads, schur, local_inverse, psi, face_map, primal_list, coarse_inverse):
    nb, nm, npl = sizes
    ng = nm * npl
    half, cases = loads.shape[2:]
    face = half // 4
    owned, coarse = coarse_inverse.shape
    group = ng * owned
    shape = jax.ShapeDtypeStruct((half, cases), F32)
    vmem = pl.BlockSpec(memory_space=pltpu.VMEM)
    smem = pl.BlockSpec(memory_space=pltpu.SMEM)
    hbm = pl.BlockSpec(memory_space=pl.ANY)
    faces = (4, face, cases)
    dma = pltpu.SemaphoreType.DMA
    scratch = (
        [pltpu.VMEM((2, half, half), F32)] * 2
        + [pltpu.VMEM((2, half, half), BF16)] * 4
        + [pltpu.VMEM((EXCH,) + faces, F32)] * 4
        + [pltpu.VMEM(faces, F32)] * 3
        + [
            pltpu.VMEM((half, cases), F32),
            pltpu.VMEM(faces, F32),
            pltpu.VMEM((2, half, 2 * cases), BF16),
            pltpu.VMEM((4, face, face), BF16),
            pltpu.VMEM((half, 3 * owned), BF16),
            pltpu.VMEM((2 * owned, half), BF16),
            pltpu.VMEM((5, owned, coarse), F32),
            pltpu.VMEM((nb + 2, owned, group), F32),
            pltpu.VMEM((nb, 3, owned, group), F32),
            pltpu.VMEM((nb * owned, group), F32),
            pltpu.VMEM((ng, owned, 128), jnp.int32),
            pltpu.VMEM((ITERS, ng, owned, cases), F32),
            pltpu.VMEM((ITERS, nb, owned, cases), F32),
            pltpu.VMEM((ITERS, nb, owned, cases), F32),
            pltpu.VMEM((2 * ITERS, ng, 1, cases), F32),
            pltpu.VMEM((2 * ITERS, nb, 1, cases), F32),
            pltpu.VMEM((1, cases), F32),
        ]
        + [dma((4,))]
        + [dma((EXCH, 4))] * 2
        + [dma((EXCH, 2))] * 2
        + [dma((4,))] * 2
        + [dma((1,))] * 4
        + [dma((ITERS,))] * 4
        + [dma((2 * ITERS,))] * 4
    )
    x, r = pl.pallas_call(
        functools.partial(kernel, sizes),
        out_shape=(shape, shape),
        in_specs=[vmem, hbm, hbm, vmem, vmem, smem, vmem],
        out_specs=(vmem, vmem),
        scratch_shapes=scratch,
        compiler_params=pltpu.CompilerParams(
            collective_id=0, has_side_effects=True, vmem_limit_bytes=56 * 1024 * 1024
        ),
        name="bddc_cg",
    )(
        loads[0, 0],
        schur[0, 0],
        local_inverse[0, 0],
        psi[0, 0],
        face_map[0, 0, 0],
        primal_list[0, 0, 0],
        coarse_inverse,
    )
    return x[None, None], r[None, None]


def solution(mesh):
    sizes = tuple(mesh.shape[axis] for axis in ("blk", "mer", "ply"))
    in_specs = (
        P("blk", "mer", "ply", None),
        P("blk", "mer", "ply", None),
        P("blk", "mer", "ply", None),
        P("blk", "mer", "ply", None),
        P("blk", "mer", "ply", None, None),
        P("blk", "mer", "ply", None),
        P(("blk", "mer", "ply"), None),
    )
    out_specs = (P("blk", "mer", "ply", None), P("blk", "mer", "ply", None))
    return jax.shard_map(
        functools.partial(local, sizes), mesh=mesh, in_specs=in_specs, out_specs=out_specs, check_vma=False
    )
```

time: 1880 us -> 187 us (0.10)
  waiting for transfers between devices: 994 us -> 0 us
  blocking collectives: 605 us -> 0 us
  Pallas kernels: 0 us -> 181 us
  starting transfers between devices: 127 us -> 0 us
  matrix products: 77.9 us -> 0 us
  local copies, waits for them, and re-layouts: 37.4 us -> 5.18 us
    psum x4 -> x0, waiting for transfers between devices: 956 us -> none  [coarse_values(): coarse_rhs = lax.psum(spread, ('blk', 'mer', 'ply'))]
    psum x7 -> x0, blocking collectives: 520 us -> none  [inner(): lax.psum(jnp.sum(weights * left * right, axis=0), ('blk', 'mer', 'ply'))]
    pallas_call x0 -> x1, Pallas kernels: none -> 181 us  [local(): pl.pallas_call(functools.partial(kernel, sizes), out_shape=(shape, shape)...]
    ppermute x52 -> x0, starting transfers between devices: 127 us -> none  [the longest x26 64.1 us: padded(): lax.ppermute(lax.slice_in_dim(block, 0, width, axis=dim), axis, backward)]
    all_gather x8 -> x0, blocking collectives: 85.2 us -> none  [product(): lax.all_gather(vec, 'ply', axis=0, tiled=True)]
    dot_general x28 -> x0, matrix products: 77.9 us -> none  [the longest x8 58 us: product(): jnp.dot(matrix, lax.all_gather(vec, 'ply', axis=0, tiled=True), precision...]
    ppermute x52 -> x0, waiting for transfers between devices: 37.7 us -> none  [the longest x26 24.1 us: padded(): lax.ppermute(lax.slice_in_dim(block, block.shape[dim] - width, None, axis...]
    gather x36 -> x0, local copies, waits for them, and re-layouts: 25.2 us -> none  [the longest x9 6.31 us: assemble(): jnp.take(meridian[0], links[2], axis=0)]
  transfers between devices with their start and end apart: 56 -> 0, of which waited for: 19 -> 0; matrix products, arithmetic and copies ran while one was open for 3% -> 0% of each run, Pallas kernels for 0% -> 0%
where the time goes in v1:
time: 187 us
  Pallas kernels  181 us (97%)
  local copies, waits for them, and re-layouts  5.18 us (3%)
    pallas_call x1, Pallas kernels, local(): pl.pallas_call(functools.partial(kernel, sizes), out_shape=(shape, shape)...  181 us
    unnamed x3, local copies, waits for them, and re-layouts  5.18 us

profile of v1, /device:TPU:1, one launch (start us, length us, event | category | flops | bytes accessed | tf_op | source)
XLA Modules:
  0.0 186.9 jit_solution(14394595403630931498)
XLA Ops:
  0.6 1.7 copy.9
  2.3 181.1 %bddc_cg.1 = (f32[768,128]{1,0:T(8,128)}, f32[768,128]{1,0:T(8,128)}) custom-call(f32[768,128]{1,0:T(8,128)} %bitcast.11, f32[768,1536]{1,0:T(8,128)} %bitcast.8, f32[768,1536]{1,0:T(8,128)} %bitcast.9, f32[768,8]{1,0:T(8,128)} %bitcast.10, s32[4,192]{1,0:T(4,128)} %bitcast.14, s32[8]{0:T(128)} %bitcast.15, f32[8,2048]{1,0:T(8,128)} %coarse_ref.1), custom_call_target="tpu_custom_call" | custom-call | tf_op jit(solution)/shard_map/bddc_cg/pallas_call | solution.py:480
  183.4 1.8 copy.12
  185.2 1.8 copy.13

commit v2 on v1

--- a/solution.py
+++ b/solution.py
@@ -45,9 +45,9 @@
     lf, sf, lhi, llo, shi, slo,
     face_tx, face_rx, own, ply_rx,
     other, pdir, sraw, acc, gvec, tb, perm, psc, pst,
-    nbr, dpad, wblk, cblk, lists,
+    fwd_tx, pmap, nbr, dpad, wblk, cblk, lists,
     co1, ytx, co2, ar1, ar2, rz_ref,
-    load_sem, face_ss, face_rs, ply_ss, ply_rs,
+    load_sem, face_ss, face_rs, ply_ss, ply_rs, fwd_ss, map_ss, map_rs,
     nbr_ss, nbr_rs, win_ss, win_rs, list_ss, list_rs,
     co1_ss, co1_rs, co2_ss, co2_rs, ar1_ss, ar1_rs, ar2_ss, ar2_rs,
 ):
@@ -74,6 +74,13 @@
     partner = (b, m, q)
     neighbour = [(b_prev, m, p), (b_next, m, p), (b, m - 1, p), (b, m + 1, p)]
     exists = [None, None, has_lo, has_hi]
+    run = nb // 2
+    place = lax.rem(b, run)
+    first = jnp.where(place < run // 2, 0, 1)
+    second = 1 - first
+    at_end = jnp.logical_or(place == 0, place == run - 1)
+    serves_end = jnp.logical_or(place == 1, place == run - 2)
+    toward_end = (jnp.where(first == 0, b_prev, b_next), m, p)
 
     def guarded(f, fn):
         if exists[f] is None:
@@ -138,6 +145,8 @@
             lax.fori_loop(0, EXCH, clear, 0)
             nbr[1 + f] = jnp.zeros(nbr.shape[1:], F32)
 
+    map_copy = remote(map_ref, pmap, map_ss.at[0], map_rs.at[0], partner)
+
     lane = lax.broadcasted_iota(jnp.int32, (owned, lists.shape[2]), 1)
     sub = lax.broadcasted_iota(jnp.int32, (owned, lists.shape[2]), 0)
     mine = jnp.zeros_like(lane)
@@ -174,9 +183,53 @@
         for f in range(4):
             guarded(f, lambda f=f: face_copy(e, f).wait_send())
 
-    def ply_copy(e, pair):
-        part = pl.ds(2 * pair, 2)
-        return remote(own.at[e, part], ply_rx.at[e, part], ply_ss.at[e, pair], ply_rs.at[e, pair], partner)
+    def ply_copy(e, f):
+        return remote(own.at[e, f], ply_rx.at[e, f], ply_ss.at[e, f], ply_rs.at[e, f], partner)
+
+    def mer_forward(e):
+        return remote(
+            fwd_tx.at[e, 0], ply_rx.at[e, 3], fwd_ss.at[e, 0], ply_rs.at[e, 3], neighbour[2]
+        )
+
+    def end_forward(e):
+        return remote(
+            fwd_tx.at[e, 1], ply_rx.at[e, second], fwd_ss.at[e, 1], ply_rs.at[e, second], toward_end
+        )
+
+    def when(condition, fn):
+        pl.when(condition)(fn)
+
+    def ply_send_mer(e):
+        ply_copy(e, 2).start()
+        when(jnp.logical_not(has_hi), lambda: ply_copy(e, 3).start())
+
+    def ply_send_cycle(e):
+        ply_copy(e, first).start()
+        when(jnp.logical_not(at_end), lambda: ply_copy(e, second).start())
+
+    def pass_mer(e):
+        ply_copy(e, 2).wait_recv()
+
+        @pl.when(has_lo)
+        def _():
+            fwd_tx[e, 0] = permute(6, ply_rx[e, 2])
+            mer_forward(e).start()
+
+    def pass_end(e):
+        ply_copy(e, first).wait_recv()
+
+        @pl.when(serves_end)
+        def _():
+            fwd_tx[e, 1] = permute(4 + first, ply_rx[e, first])
+            end_forward(e).start()
+
+    def ply_sent(e):
+        ply_copy(e, 2).wait_send()
+        when(jnp.logical_not(has_hi), lambda: ply_copy(e, 3).wait_send())
+        ply_copy(e, first).wait_send()
+        when(jnp.logical_not(at_end), lambda: ply_copy(e, second).wait_send())
+        when(has_lo, lambda: mer_forward(e).wait_send())
+        when(serves_end, lambda: end_forward(e).wait_send())
 
     def batch(buffer, index, count, send, recv):
         block = buffer.at[index, pl.ds(0, count - 1)]
@@ -205,14 +258,15 @@
         tb[side, part, pl.ds(0, cases)] = hi
         tb[side, part, pl.ds(cases, cases)] = lo
 
-    def product(hi, lo, side):
-        both = dot(hi[side], tb[side])
-        small = dot(lo[side], tb[side, :, pl.ds(0, cases)])
+    def product(hi, lo, side, pair):
+        part = pl.ds(2 * pair * face, 2 * face)
+        both = dot(hi[side, :, part], tb[side, part, :])
+        small = dot(lo[side, :, part], tb[side, part, pl.ds(0, cases)])
         return (both[:, :cases] + both[:, cases:]) + small
 
     pl.semaphore_wait(barrier, ng - 1 + nb - 1)
 
-    for f in (0, 1, 2, 3):
+    for f in (2, 3, 0, 1):
         face_send(0, f, loads_ref[pl.ds(f * face, face), :])
 
     slot_there = [2, 1, 4, 3]
@@ -223,18 +277,20 @@
 
     for f in range(4):
         guarded(f, lambda f=f: nbr_copy(f).start())
+    map_copy.start()
     nbr[0] = coarse_ref[...]
     spread(ng, mp, mp_device, lambda _: lists.at[mp], lists.at[mp], list_ss.at[0], list_rs.at[0])
 
-    psi = psi_ref[...]
-    psi_hi, psi_lo = halves(psi)
-    psi_hi = psi_hi.astype(F32)
-    psc[...] = jnp.concatenate([psi_hi, psi_hi, psi_lo.astype(F32)], axis=1).astype(BF16)
-    pick_r = lax.broadcasted_iota(jnp.int32, (2 * owned, 3 * owned), 0)
-    pick_c = lax.broadcasted_iota(jnp.int32, (2 * owned, 3 * owned), 1)
-    want = jnp.where(pick_r < owned, pick_r, pick_r + owned)
-    pick = jnp.where(want == pick_c, 1.0, 0.0).astype(BF16)
-    pst[...] = lax.dot_general(pick, psc[...], NT, preferred_element_type=F32).astype(BF16)
+    psi_hi, psi_lo = halves(psi_ref[...])
+    psi_hi, psi_lo = psi_hi.astype(F32), psi_lo.astype(F32)
+    pst[...] = jnp.concatenate([psi_hi, psi_lo], axis=0).astype(BF16)
+    three = jnp.concatenate([psi_hi, psi_hi, psi_lo], axis=0).astype(BF16)
+    eye_r = lax.broadcasted_iota(jnp.int32, (3 * owned, 3 * owned), 0)
+    eye_c = lax.broadcasted_iota(jnp.int32, (3 * owned, 3 * owned), 1)
+    eye = jnp.where(eye_r == eye_c, 1.0, 0.0).astype(BF16)
+    psc[...] = lax.dot_general(
+        three, eye, (((0,), (0,)), ((), ())), preferred_element_type=F32
+    ).astype(BF16)
 
     def split_matrix(source, hi, lo):
         def step(i, carry):
@@ -285,14 +341,22 @@
     wblk[b] = dpad[pl.ds(b, 3)]
     spread(nb, b, blk_device, lambda peer: dpad.at[pl.ds(peer, 3)], wblk.at[b], win_ss.at[0], win_rs.at[0])
 
-    for f in (2, 3, 0, 1):
+    def first_residual(f):
         face_wait(0, f)
         value = loads_ref[pl.ds(f * face, face), :] + face_rx[0, f]
         own[0, f] = value
         r_ref[pl.ds(f * face, face), :] = value
         other[f] = jnp.zeros((face, cases), F32)
-        if f in (3, 1):
-            ply_copy(0, f // 2).start()
+
+    first_residual(2)
+    first_residual(3)
+    ply_send_mer(0)
+    first_residual(0)
+    first_residual(1)
+    ply_send_cycle(0)
+    map_copy.wait_recv()
+    for f in range(3):
+        perm[4 + f] = jnp.where(rows == pmap[f : f + 1, :], 1.0, 0.0).astype(BF16)
     x_ref[...] = jnp.zeros_like(x_ref)
     pdir[...] = jnp.zeros_like(pdir)
     sraw[...] = jnp.zeros_like(sraw)
@@ -317,6 +381,7 @@
     remote(block, block, list_ss.at[0], list_rs.at[0], partner).wait_send()
     block = wblk.at[pl.ds(0, nb - 1)]
     remote(block, block, win_ss.at[0], win_rs.at[0], partner).wait_send()
+    map_copy.wait_send()
     faces_sent(0)
 
     def iteration(it, alpha):
@@ -331,7 +396,10 @@
         terms = parts[:owned, :cases] + parts[:owned, cases:] + parts[owned:, :cases]
         co1[it, mp] = terms
         spread(ng, mp, mp_device, lambda _: co1.at[it, mp], co1.at[it, mp], co1_ss.at[it], co1_rs.at[it])
-        acc[...] = product(lhi, llo, 0)
+        pass_mer(e1 - 1)
+        pass_end(e1 - 1)
+        acc[...] = product(lhi, llo, 0, 1)
+        acc[...] += product(lhi, llo, 0, 0)
 
         batch(co1, it, ng, co1_ss.at[it], co1_rs.at[it]).wait_recv()
         y = jnp.dot(
@@ -347,13 +415,15 @@
             fetches[3].wait()
             split_matrix(sf, shi, slo)
 
-        for f in (2, 3, 0, 1):
-            if f in (2, 0):
-                ply_copy(e1 - 1, f // 2).wait_recv()
-            value = other[f] + alpha * ply_rx[e1 - 1, f]
-            other[f] = value
-            store_split(1, f, weight[f] * value)
-        acc[...] += product(lhi, llo, 1)
+        ply_copy(e1 - 1, 3).wait_recv()
+        for pair in (1, 0):
+            if pair == 0:
+                ply_copy(e1 - 1, second).wait_recv()
+            for f in (2 * pair, 2 * pair + 1):
+                value = other[f] + alpha * ply_rx[e1 - 1, f]
+                other[f] = value
+                store_split(1, f, weight[f] * value)
+            acc[...] += product(lhi, llo, 1, pair)
 
         batch(co2, it, nb, co2_ss.at[it], co2_rs.at[it]).wait_recv()
         picked = jnp.sum(co2[it], axis=0)
@@ -362,7 +432,7 @@
         acc[...] += dot(psc[...], stack)
 
         partial = jnp.zeros((8, cases), F32)
-        for f in (0, 1, 2, 3):
+        for f in (2, 3, 0, 1):
             part = pl.ds(f * face, face)
             value = weight[f] * acc[part, :]
             gvec[f] = value
@@ -370,16 +440,24 @@
             partial += jnp.sum((value * r_ref[part, :]).reshape(face // 8, 8, cases), axis=0)
         reduce_first(k1, jnp.sum(partial, axis=0, keepdims=True))
 
-        for f in (2, 3, 0, 1):
+        def assembled(f):
             face_wait(e1, f)
             value = gvec[f] + face_rx[e1, f]
             own[e1, f] = value
-            if f in (3, 1):
-                ply_copy(e1, f // 2).start()
             store_split(0, f, value)
+
+        assembled(2)
+        assembled(3)
+        ply_send_mer(e1)
+
+        acc[...] = product(shi, slo, 0, 1)
+        assembled(0)
+        assembled(1)
+        ply_send_cycle(e1)
+        pass_mer(e1)
         reduce_second(k1)
-
-        acc[...] = product(shi, slo, 0)
+        acc[...] += product(shi, slo, 0, 0)
+        pass_end(e1)
         rz = reduce_end(k1)
         beta = jnp.where(it == 0, 0.0, rz / rz_ref[...])
         rz_ref[...] = rz
@@ -389,37 +467,37 @@
         batch(co2, it, nb, co2_ss.at[it], co2_rs.at[it]).wait_send()
         reduce_sent(k1)
         faces_sent(e1)
-        for pair in range(2):
-            ply_copy(e1 - 1, pair).wait_send()
-        for f in (2, 3, 0, 1):
-            if f in (2, 0):
-                ply_copy(e1, f // 2).wait_recv()
-            store_split(1, f, ply_rx[e1, f])
-        acc[...] += product(shi, slo, 1)
+        ply_sent(e1 - 1)
+        ply_copy(e1, 3).wait_recv()
+        for pair in (1, 0):
+            if pair == 0:
+                ply_copy(e1, second).wait_recv()
+            for f in (2 * pair, 2 * pair + 1):
+                store_split(1, f, ply_rx[e1, f])
+            acc[...] += product(shi, slo, 1, pair)
         partial = jnp.zeros((8, cases), F32)
-        for f in (0, 1, 2, 3):
+        for f in range(4):
             value = acc[pl.ds(f * face, face), :] + beta * sraw[f]
             sraw[f] = value
-            face_send(e2, f, value)
             partial += jnp.sum((value * pdir[f]).reshape(face // 8, 8, cases), axis=0)
         reduce_first(k2, jnp.sum(partial, axis=0, keepdims=True))
-
-        def assembled(f):
+        for f in (2, 3, 0, 1):
+            face_send(e2, f, sraw[f])
+
+        more = it + 1 < ITERS
+
+        def image(f):
             face_wait(e2, f)
             own[e2, f] = sraw[f] + face_rx[e2, f]
-            if f in (3, 1):
-
-                @pl.when(it + 1 < ITERS)
-                def _():
-                    ply_copy(e2, f // 2).start()
-
-        assembled(2)
-        assembled(3)
+
+        image(2)
+        image(3)
+        when(more, lambda: ply_send_mer(e2))
         reduce_second(k2)
-        assembled(0)
-        assembled(1)
-        for pair in range(2):
-            ply_copy(e1, pair).wait_send()
+        image(0)
+        image(1)
+        when(more, lambda: ply_send_cycle(e2))
+        ply_sent(e1)
         alpha = rz / reduce_end(k2)
         for f in range(4):
             part = pl.ds(f * face, face)
@@ -430,6 +508,17 @@
         return -alpha
 
     lax.fori_loop(0, ITERS, iteration, jnp.ones((1, cases), F32))
+
+
+def deliver(x_ref, r_ref, x_out, r_out, sem):
+    copies = [
+        pltpu.make_async_copy(x_ref, x_out, sem.at[0]),
+        pltpu.make_async_copy(r_ref, r_out, sem.at[1]),
+    ]
+    for copy in copies:
+        copy.start()
+    for copy in copies:
+        copy.wait()
 
 
 def local(sizes, loads, schur, local_inverse, psi, face_map, primal_list, coarse_inverse):
@@ -454,9 +543,11 @@
             pltpu.VMEM((half, cases), F32),
             pltpu.VMEM(faces, F32),
             pltpu.VMEM((2, half, 2 * cases), BF16),
-            pltpu.VMEM((4, face, face), BF16),
+            pltpu.VMEM((7, face, face), BF16),
             pltpu.VMEM((half, 3 * owned), BF16),
             pltpu.VMEM((2 * owned, half), BF16),
+            pltpu.VMEM((EXCH, 2, face, cases), F32),
+            pltpu.VMEM((4, face), jnp.int32),
             pltpu.VMEM((5, owned, coarse), F32),
             pltpu.VMEM((nb + 2, owned, group), F32),
             pltpu.VMEM((nb, 3, owned, group), F32),
@@ -471,7 +562,9 @@
         ]
         + [dma((4,))]
         + [dma((EXCH, 4))] * 2
-        + [dma((EXCH, 2))] * 2
+        + [dma((EXCH, 4))] * 2
+        + [dma((EXCH, 2))]
+        + [dma((1,))] * 2
         + [dma((4,))] * 2
         + [dma((1,))] * 4
         + [dma((ITERS,))] * 4
@@ -491,11 +584,19 @@
         loads[0, 0],
         schur[0, 0],
         local_inverse[0, 0],
-        psi[0, 0],
+        psi[0, 0].T,
         face_map[0, 0, 0],
         primal_list[0, 0, 0],
         coarse_inverse,
     )
+    x, r = pl.pallas_call(
+        deliver,
+        out_shape=(shape, shape),
+        in_specs=[hbm, hbm],
+        out_specs=(hbm, hbm),
+        scratch_shapes=[dma((2,))],
+        name="deliver",
+    )(x, r)
     return x[None, None], r[None, None]
 
 

time: 187 us -> 201 us (1.075)
  Pallas kernels: 181 us -> 201 us
  local copies, waits for them, and re-layouts: 5.18 us -> 0 us
    pallas_call x0 -> x1, Pallas kernels: none -> 24.9 us  [local(): pl.pallas_call(deliver, out_shape=(shape, shape), in_specs=[hbm, hbm], ou...]
    pallas_call x1, Pallas kernels: 181 us -> 176 us  [local(): pl.pallas_call(functools.partial(kernel, sizes), out_shape=(shape, shape)...]
    unnamed x3 -> x0, local copies, waits for them, and re-layouts: 5.18 us -> none
where the time goes in v2:
time: 201 us
  Pallas kernels  201 us (100%)
    pallas_call x1, Pallas kernels, local(): pl.pallas_call(functools.partial(kernel, sizes), out_shape=(shape, shape)...  176 us
    pallas_call x1, Pallas kernels, local(): pl.pallas_call(deliver, out_shape=(shape, shape), in_specs=[hbm, hbm], ou...  24.9 us

profile of v2, /device:TPU:1, one launch (start us, length us, event | category | flops | bytes accessed | tf_op | source)
XLA Modules:
  0.0 201.3 jit_solution(180116792040896509)
XLA Ops:
  0.6 175.7 %bddc_cg.1 = (f32[768,128]{1,0:T(8,128)}, f32[768,128]{1,0:T(8,128)}) custom-call(f32[768,128]{1,0:T(8,128)} %bitcast.12, f32[768,1536]{1,0:T(8,128)} %bitcast.10, f32[768,1536]{1,0:T(8,128)} %bitcast.11, f32[8,768]{1,0:T(8,128)} %bitcast.13, s32[4,192]{1,0:T(4,128)} %bitcast.14, s32[8]{0:T(128)} %bitcast.15, f32[8,2048]{1,0:T(8,128)} %coarse_ref.1), custom_call_target="tpu_custom_call" | custom-call | tf_op jit(solution)/shard_map/bddc_cg/pallas_call | solution.py:573
  176.3 24.9 %deliver.1 = (f32[768,128]{1,0:T(8,128)}, f32[768,128]{1,0:T(8,128)}) custom-call(f32[768,128]{1,0:T(8,128)} %get-tuple-element.6.x_ref, f32[768,128]{1,0:T(8,128)} %get-tuple-element.7.r_ref), custom_call_target="tpu_custom_call" | custom-call | tf_op jit(solution)/shard_map/deliver/pallas_call | solution.py:592

commit v3 on v2

--- a/solution.py
+++ b/solution.py
@@ -44,12 +44,12 @@
     x_ref, r_ref,
     lf, sf, lhi, llo, shi, slo,
     face_tx, face_rx, own, ply_rx,
-    other, pdir, sraw, acc, gvec, tb, perm, psc, pst,
+    pdir, simg, mdir, upre, raw, acc, tb, perm, psc, pst,
     fwd_tx, pmap, nbr, dpad, wblk, cblk, lists,
-    co1, ytx, co2, ar1, ar2, rz_ref,
+    sums, co1, ytx, co2, rz_ref, pap_ref,
     load_sem, face_ss, face_rs, ply_ss, ply_rs, fwd_ss, map_ss, map_rs,
     nbr_ss, nbr_rs, win_ss, win_rs, list_ss, list_rs,
-    co1_ss, co1_rs, co2_ss, co2_rs, ar1_ss, ar1_rs, ar2_ss, ar2_rs,
+    co1_ss, co1_rs, co2_ss, co2_rs,
 ):
     nb, nm, npl = sizes
     ng = nm * npl
@@ -88,19 +88,12 @@
         else:
             pl.when(exists[f])(fn)
 
-    def mp_device(index):
-        return (b, lax.div(index, npl), lax.rem(index, npl))
-
-    def blk_device(index):
-        return (index, m, p)
-
-    def spread(count, me, device_of, src_of, dst, send, recv):
-        def step(j, carry):
-            peer = lax.rem(me + j, count)
-            remote(src_of(peer), dst, send, recv, device_of(peer)).start()
-            return carry
-
-        lax.fori_loop(1, count, step, 0)
+    mp_devices = [(b, i // npl, i % npl) for i in range(ng)]
+    blk_devices = [(i, m, p) for i in range(nb)]
+
+    def spread(me, devices, src_of, dst, send, recv):
+        for i, device in enumerate(devices):
+            pl.when(me != i)(lambda: remote(src_of(i), dst, send, recv, device).start())
 
     def fetch(index, source, side, target):
         column = pl.multiple_of(side * half, 128)
@@ -119,16 +112,15 @@
 
     barrier = pltpu.get_barrier_semaphore()
 
-    def greet(count, me, device_of):
-        def step(j, carry):
-            peer = lax.rem(me + j, count)
-            pl.semaphore_signal(barrier, inc=1, device_id=device_of(peer), device_id_type=MESH)
-            return carry
-
-        lax.fori_loop(1, count, step, 0)
-
-    greet(ng, mp, mp_device)
-    greet(nb, b, blk_device)
+    def greet(me, devices):
+        for i, device in enumerate(devices):
+
+            @pl.when(me != i)
+            def _():
+                pl.semaphore_signal(barrier, inc=1, device_id=device, device_id_type=MESH)
+
+    greet(mp, mp_devices)
+    greet(b, blk_devices)
 
     rows = lax.broadcasted_iota(jnp.int32, (face, face), 0)
     for f in range(4):
@@ -235,22 +227,47 @@
         block = buffer.at[index, pl.ds(0, count - 1)]
         return remote(block, block, send, recv, partner)
 
-    def reduce_first(k, value):
-        ar1[k, mp] = value
-        spread(ng, mp, mp_device, lambda _: ar1.at[k, mp], ar1.at[k, mp], ar1_ss.at[k], ar1_rs.at[k])
-
-    def reduce_second(k):
-        batch(ar1, k, ng, ar1_ss.at[k], ar1_rs.at[k]).wait_recv()
-        ar2[k, b] = jnp.sum(ar1[k], axis=0)
-        spread(nb, b, blk_device, lambda _: ar2.at[k, b], ar2.at[k, b], ar2_ss.at[k], ar2_rs.at[k])
-
-    def reduce_end(k):
-        batch(ar2, k, nb, ar2_ss.at[k], ar2_rs.at[k]).wait_recv()
-        return jnp.sum(ar2[k], axis=0)
-
-    def reduce_sent(k):
-        batch(ar1, k, ng, ar1_ss.at[k], ar1_rs.at[k]).wait_send()
-        batch(ar2, k, nb, ar2_ss.at[k], ar2_rs.at[k]).wait_send()
+    def group_first(it, terms):
+        co1[it, mp, pl.ds(0, owned)] = terms
+        co1[it, mp, pl.ds(owned, 8)] = sums[...]
+        spread(mp, mp_devices, lambda _: co1.at[it, mp], co1.at[it, mp], co1_ss.at[it], co1_rs.at[it])
+
+    def group_second(it, coarse):
+        batch(co1, it, ng, co1_ss.at[it], co1_rs.at[it]).wait_recv()
+        if coarse:
+            y = jnp.dot(
+                cblk[...],
+                co1[it, :, pl.ds(0, owned)].reshape(ng * owned, cases),
+                precision=HIGH,
+                preferred_element_type=F32,
+            )
+            ytx[it, :, pl.ds(0, owned)] = y.reshape(nb, owned, cases)
+        else:
+            ytx[it, :, pl.ds(0, owned)] = jnp.zeros((nb, owned, cases), F32)
+        inner = jnp.sum(co1[it, :, pl.ds(owned, 8)], axis=0)
+        ytx[it, :, pl.ds(owned, 8)] = jnp.broadcast_to(inner[None], (nb, 8, cases))
+        spread(b, blk_devices, lambda i: ytx.at[it, i], co2.at[it, b], co2_ss.at[it], co2_rs.at[it])
+        co2[it, b] = ytx[it, b]
+
+    def group_end(it):
+        batch(co2, it, nb, co2_ss.at[it], co2_rs.at[it]).wait_recv()
+        total = jnp.sum(co2[it], axis=0)
+        return total[:owned], total[owned : owned + 1], total[owned + 1 : owned + 2], total[owned + 2 : owned + 3]
+
+    def group_sent(it):
+        batch(co1, it, ng, co1_ss.at[it], co1_rs.at[it]).wait_send()
+        batch(co2, it, nb, co2_ss.at[it], co2_rs.at[it]).wait_send()
+
+    def rows_sum(value):
+        return jnp.sum(value.reshape(face // 8, 8, cases), axis=0)
+
+    def put_sums(parts):
+        flat = [jnp.sum(part, axis=0, keepdims=True) for part in parts]
+        index = lax.broadcasted_iota(jnp.int32, (8, cases), 0)
+        out = jnp.zeros((8, cases), F32)
+        for i, part in enumerate(flat):
+            out = jnp.where(index == i, part, out)
+        sums[...] = out
 
     def store_split(side, f, value):
         hi, lo = halves(value)
@@ -267,7 +284,8 @@
     pl.semaphore_wait(barrier, ng - 1 + nb - 1)
 
     for f in (2, 3, 0, 1):
-        face_send(0, f, loads_ref[pl.ds(f * face, face), :])
+        raw[f] = loads_ref[pl.ds(f * face, face), :]
+        face_send(0, f, raw[f])
 
     slot_there = [2, 1, 4, 3]
 
@@ -279,7 +297,7 @@
         guarded(f, lambda f=f: nbr_copy(f).start())
     map_copy.start()
     nbr[0] = coarse_ref[...]
-    spread(ng, mp, mp_device, lambda _: lists.at[mp], lists.at[mp], list_ss.at[0], list_rs.at[0])
+    spread(mp, mp_devices, lambda _: lists.at[mp], lists.at[mp], list_ss.at[0], list_rs.at[0])
 
     psi_hi, psi_lo = halves(psi_ref[...])
     psi_hi, psi_lo = psi_hi.astype(F32), psi_lo.astype(F32)
@@ -339,186 +357,169 @@
         block = (j - 1) % nb
         dpad[j] = named[:, block * group : (block + 1) * group]
     wblk[b] = dpad[pl.ds(b, 3)]
-    spread(nb, b, blk_device, lambda peer: dpad.at[pl.ds(peer, 3)], wblk.at[b], win_ss.at[0], win_rs.at[0])
-
-    def first_residual(f):
-        face_wait(0, f)
-        value = loads_ref[pl.ds(f * face, face), :] + face_rx[0, f]
-        own[0, f] = value
-        r_ref[pl.ds(f * face, face), :] = value
-        other[f] = jnp.zeros((face, cases), F32)
-
-    first_residual(2)
-    first_residual(3)
-    ply_send_mer(0)
-    first_residual(0)
-    first_residual(1)
-    ply_send_cycle(0)
+    spread(b, blk_devices, lambda peer: dpad.at[pl.ds(peer, 3)], wblk.at[b], win_ss.at[0], win_rs.at[0])
+
     map_copy.wait_recv()
     for f in range(3):
         perm[4 + f] = jnp.where(rows == pmap[f : f + 1, :], 1.0, 0.0).astype(BF16)
-    x_ref[...] = jnp.zeros_like(x_ref)
-    pdir[...] = jnp.zeros_like(pdir)
-    sraw[...] = jnp.zeros_like(sraw)
+    for state in (x_ref, r_ref, pdir, simg, mdir, upre, pap_ref, sums):
+        state[...] = jnp.zeros_like(state)
     rz_ref[...] = jnp.ones_like(rz_ref)
 
-    block = lists.at[pl.ds(0, ng - 1)]
-    remote(block, block, list_ss.at[0], list_rs.at[0], partner).wait_recv()
-    names = lists[:, :, pl.ds(0, group)].reshape(group, group)
-    column = lax.broadcasted_iota(jnp.int32, (group, group), 1)
-    block = wblk.at[pl.ds(0, nb - 1)]
-    remote(block, block, win_ss.at[0], win_rs.at[0], partner).wait_recv()
-    total = jnp.zeros((nb * owned, group), F32)
-    for j, start in enumerate((b_prev, b, b_next)):
-        hot = jnp.where(names == column + start * group, 1.0, 0.0).astype(F32)
-        window = wblk[:, j].reshape(nb * owned, group)
-        total += lax.dot_general(window, hot, NT, precision=HIGH, preferred_element_type=F32)
-    cblk[...] = total
-
-    for f in range(4):
-        guarded(f, lambda f=f: nbr_copy(f).wait_send())
-    block = lists.at[pl.ds(0, ng - 1)]
-    remote(block, block, list_ss.at[0], list_rs.at[0], partner).wait_send()
-    block = wblk.at[pl.ds(0, nb - 1)]
-    remote(block, block, win_ss.at[0], win_rs.at[0], partner).wait_send()
-    map_copy.wait_send()
-    faces_sent(0)
-
-    def iteration(it, alpha):
-        e1 = 1 + 2 * it
-        e2 = 2 + 2 * it
-        k1 = 2 * it
-        k2 = 2 * it + 1
-
+    def coarse_block():
+        block = lists.at[pl.ds(0, ng - 1)]
+        remote(block, block, list_ss.at[0], list_rs.at[0], partner).wait_recv()
+        names = lists[:, :, pl.ds(0, group)].reshape(group, group)
+        column = lax.broadcasted_iota(jnp.int32, (group, group), 1)
+        block = wblk.at[pl.ds(0, nb - 1)]
+        remote(block, block, win_ss.at[0], win_rs.at[0], partner).wait_recv()
+        total = jnp.zeros((nb * owned, group), F32)
+        for j, start in enumerate((b_prev, b, b_next)):
+            hot = jnp.where(names == column + start * group, 1.0, 0.0).astype(F32)
+            window = wblk[:, j].reshape(nb * owned, group)
+            total += lax.dot_general(window, hot, NT, precision=HIGH, preferred_element_type=F32)
+        cblk[...] = total
         for f in range(4):
-            store_split(0, f, weight[f] * r_ref[pl.ds(f * face, face), :])
-        parts = dot(pst[...], tb[0])
-        terms = parts[:owned, :cases] + parts[:owned, cases:] + parts[owned:, :cases]
-        co1[it, mp] = terms
-        spread(ng, mp, mp_device, lambda _: co1.at[it, mp], co1.at[it, mp], co1_ss.at[it], co1_rs.at[it])
-        pass_mer(e1 - 1)
-        pass_end(e1 - 1)
-        acc[...] = product(lhi, llo, 0, 1)
-        acc[...] += product(lhi, llo, 0, 0)
-
-        batch(co1, it, ng, co1_ss.at[it], co1_rs.at[it]).wait_recv()
-        y = jnp.dot(
-            cblk[...], co1[it].reshape(group, cases), precision=HIGH, preferred_element_type=F32
-        )
-        ytx[it] = y.reshape(nb, owned, cases)
-        spread(nb, b, blk_device, lambda peer: ytx.at[it, peer], co2.at[it, b], co2_ss.at[it], co2_rs.at[it])
-        co2[it, b] = ytx[it, b]
-
-        @pl.when(it == 0)
-        def _():
-            fetches[2].wait()
-            fetches[3].wait()
-            split_matrix(sf, shi, slo)
-
-        ply_copy(e1 - 1, 3).wait_recv()
+            guarded(f, lambda f=f: nbr_copy(f).wait_send())
+        block = lists.at[pl.ds(0, ng - 1)]
+        remote(block, block, list_ss.at[0], list_rs.at[0], partner).wait_send()
+        block = wblk.at[pl.ds(0, nb - 1)]
+        remote(block, block, win_ss.at[0], win_rs.at[0], partner).wait_send()
+        map_copy.wait_send()
+
+    def assemble(e, pair, weights, ply):
+        for f in (2 * pair, 2 * pair + 1):
+            face_wait(e, f)
+            value = raw[f] + face_rx[e, f]
+            own[e, f] = value
+        if ply and pair:
+            ply_send_mer(e)
+        elif ply:
+            ply_send_cycle(e)
+        if ply:
+            for f in (2 * pair, 2 * pair + 1):
+                value = own[e, f]
+                store_split(0, f, value if weights is None else weights[f] * value)
+
+    def exchange(e, hi, lo, weights, begin, middle):
+        assemble(e, 1, weights, True)
+        acc[...] = product(hi, lo, 0, 1)
+        assemble(e, 0, weights, True)
+        begin()
+        pass_mer(e)
+        acc[...] += product(hi, lo, 0, 0)
+        pass_end(e)
+        middle()
+        ply_copy(e, 3).wait_recv()
         for pair in (1, 0):
             if pair == 0:
-                ply_copy(e1 - 1, second).wait_recv()
+                ply_copy(e, second).wait_recv()
             for f in (2 * pair, 2 * pair + 1):
-                value = other[f] + alpha * ply_rx[e1 - 1, f]
-                other[f] = value
-                store_split(1, f, weight[f] * value)
-            acc[...] += product(lhi, llo, 1, pair)
-
-        batch(co2, it, nb, co2_ss.at[it], co2_rs.at[it]).wait_recv()
-        picked = jnp.sum(co2[it], axis=0)
+                value = ply_rx[e, f]
+                store_split(1, f, value if weights is None else weights[f] * value)
+            acc[...] += product(hi, lo, 1, pair)
+
+    def steps(it, rz, energy, cross):
+        beta = jnp.where(it <= 1, 0.0, rz / rz_ref[...])
+        pap = (energy + 2.0 * beta * cross) + beta * beta * pap_ref[...]
+        alpha = jnp.where(it == 0, -1.0, rz / pap)
+
+        @pl.when(it > 0)
+        def _():
+            rz_ref[...] = rz
+            pap_ref[...] = pap
+
+        return alpha, beta
+
+    def advance(e, alpha, beta):
+        for f in range(4):
+            part = pl.ds(f * face, face)
+            value = own[e, f] + beta * simg[f]
+            simg[f] = value
+            r_ref[part, :] -= alpha * value
+
+        @pl.when(e > 0)
+        def _():
+            for f in range(4):
+                value = own[e - 1, f] + beta * pdir[f]
+                pdir[f] = value
+                x_ref[pl.ds(f * face, face), :] += alpha * value
+
+    def iteration(it, carry):
+        e1 = 2 * it
+        e2 = e1 + 1
+
+        def begin():
+            parts = dot(pst[...], tb[0])
+            group_first(it, parts[:owned, :cases] + parts[:owned, cases:] + parts[owned:, :cases])
+
+        def middle():
+            @pl.when(it == 0)
+            def _():
+                coarse_block()
+
+            group_second(it, True)
+
+            @pl.when(it == 0)
+            def _():
+                fetches[2].wait()
+                fetches[3].wait()
+                split_matrix(sf, shi, slo)
+
+        exchange(e1, lhi, llo, weight, begin, middle)
+        picked, rz, energy, cross = group_end(it)
         pick_hi = picked.astype(BF16).astype(F32)
         stack = jnp.concatenate([pick_hi, picked - pick_hi, pick_hi], axis=0).astype(BF16)
         acc[...] += dot(psc[...], stack)
-
-        partial = jnp.zeros((8, cases), F32)
+        alpha, beta = steps(it, rz, energy, cross)
         for f in (2, 3, 0, 1):
-            part = pl.ds(f * face, face)
-            value = weight[f] * acc[part, :]
-            gvec[f] = value
-            face_send(e1, f, value)
-            partial += jnp.sum((value * r_ref[part, :]).reshape(face // 8, 8, cases), axis=0)
-        reduce_first(k1, jnp.sum(partial, axis=0, keepdims=True))
-
-        def assembled(f):
-            face_wait(e1, f)
-            value = gvec[f] + face_rx[e1, f]
-            own[e1, f] = value
-            store_split(0, f, value)
-
-        assembled(2)
-        assembled(3)
-        ply_send_mer(e1)
-
-        acc[...] = product(shi, slo, 0, 1)
-        assembled(0)
-        assembled(1)
-        ply_send_cycle(e1)
-        pass_mer(e1)
-        reduce_second(k1)
-        acc[...] += product(shi, slo, 0, 0)
-        pass_end(e1)
-        rz = reduce_end(k1)
-        beta = jnp.where(it == 0, 0.0, rz / rz_ref[...])
-        rz_ref[...] = rz
-        for f in range(4):
-            pdir[f] = own[e1, f] + beta * pdir[f]
-        batch(co1, it, ng, co1_ss.at[it], co1_rs.at[it]).wait_send()
-        batch(co2, it, nb, co2_ss.at[it], co2_rs.at[it]).wait_send()
-        reduce_sent(k1)
-        faces_sent(e1)
-        ply_sent(e1 - 1)
-        ply_copy(e1, 3).wait_recv()
-        for pair in (1, 0):
-            if pair == 0:
-                ply_copy(e1, second).wait_recv()
-            for f in (2 * pair, 2 * pair + 1):
-                store_split(1, f, ply_rx[e1, f])
-            acc[...] += product(shi, slo, 1, pair)
+            change = acc[pl.ds(f * face, face), :] + beta * mdir[f]
+            mdir[f] = change
+            value = upre[f] - alpha * change
+            upre[f] = value
+            value = weight[f] * value
+            raw[f] = value
+            face_send(e2, f, value)
+        advance(e1, alpha, beta)
         partial = jnp.zeros((8, cases), F32)
         for f in range(4):
-            value = acc[pl.ds(f * face, face), :] + beta * sraw[f]
-            sraw[f] = value
-            partial += jnp.sum((value * pdir[f]).reshape(face // 8, 8, cases), axis=0)
-        reduce_first(k2, jnp.sum(partial, axis=0, keepdims=True))
+            partial += rows_sum(raw[f] * r_ref[pl.ds(f * face, face), :])
+        faces_sent(e1)
+        ply_sent(e1)
+        group_sent(it)
+
+        exchange(e2, shi, slo, None, lambda: None, lambda: None)
         for f in (2, 3, 0, 1):
-            face_send(e2, f, sraw[f])
-
-        more = it + 1 < ITERS
-
-        def image(f):
-            face_wait(e2, f)
-            own[e2, f] = sraw[f] + face_rx[e2, f]
-
-        image(2)
-        image(3)
-        when(more, lambda: ply_send_mer(e2))
-        reduce_second(k2)
-        image(0)
-        image(1)
-        when(more, lambda: ply_send_cycle(e2))
-        ply_sent(e1)
-        alpha = rz / reduce_end(k2)
+            value = acc[pl.ds(f * face, face), :]
+            raw[f] = value
+            face_send(e2 + 1, f, value)
+        energy = jnp.zeros((8, cases), F32)
+        cross = jnp.zeros((8, cases), F32)
         for f in range(4):
-            part = pl.ds(f * face, face)
-            x_ref[part, :] += alpha * pdir[f]
-            r_ref[part, :] -= alpha * own[e2, f]
-        reduce_sent(k2)
+            energy += rows_sum(raw[f] * own[e2, f])
+            cross += rows_sum(raw[f] * pdir[f])
+        put_sums((partial, energy, cross))
         faces_sent(e2)
-        return -alpha
-
-    lax.fori_loop(0, ITERS, iteration, jnp.ones((1, cases), F32))
-
-
-def deliver(x_ref, r_ref, x_out, r_out, sem):
-    copies = [
-        pltpu.make_async_copy(x_ref, x_out, sem.at[0]),
-        pltpu.make_async_copy(r_ref, r_out, sem.at[1]),
-    ]
-    for copy in copies:
-        copy.start()
-    for copy in copies:
-        copy.wait()
+        ply_sent(e2)
+        return carry
+
+    lax.fori_loop(0, ITERS, iteration, 0)
+
+    last = EXCH - 1
+    group_first(ITERS, jnp.zeros((owned, cases), F32))
+    assemble(last, 1, None, False)
+    group_second(ITERS, False)
+    assemble(last, 0, None, False)
+    _, rz, energy, cross = group_end(ITERS)
+    alpha, beta = steps(ITERS, rz, energy, cross)
+    advance(last, alpha, beta)
+    faces_sent(last)
+    group_sent(ITERS)
+
+
+def deliver(x_ref, r_ref, x_out, r_out):
+    x_out[...] = x_ref[...]
+    r_out[...] = r_ref[...]
 
 
 def local(sizes, loads, schur, local_inverse, psi, face_map, primal_list, coarse_inverse):
@@ -538,10 +539,9 @@
         [pltpu.VMEM((2, half, half), F32)] * 2
         + [pltpu.VMEM((2, half, half), BF16)] * 4
         + [pltpu.VMEM((EXCH,) + faces, F32)] * 4
-        + [pltpu.VMEM(faces, F32)] * 3
+        + [pltpu.VMEM(faces, F32)] * 5
         + [
             pltpu.VMEM((half, cases), F32),
-            pltpu.VMEM(faces, F32),
             pltpu.VMEM((2, half, 2 * cases), BF16),
             pltpu.VMEM((7, face, face), BF16),
             pltpu.VMEM((half, 3 * owned), BF16),
@@ -553,11 +553,11 @@
             pltpu.VMEM((nb, 3, owned, group), F32),
             pltpu.VMEM((nb * owned, group), F32),
             pltpu.VMEM((ng, owned, 128), jnp.int32),
-            pltpu.VMEM((ITERS, ng, owned, cases), F32),
-            pltpu.VMEM((ITERS, nb, owned, cases), F32),
-            pltpu.VMEM((ITERS, nb, owned, cases), F32),
-            pltpu.VMEM((2 * ITERS, ng, 1, cases), F32),
-            pltpu.VMEM((2 * ITERS, nb, 1, cases), F32),
+            pltpu.VMEM((8, cases), F32),
+            pltpu.VMEM((ITERS + 1, ng, owned + 8, cases), F32),
+            pltpu.VMEM((ITERS + 1, nb, owned + 8, cases), F32),
+            pltpu.VMEM((ITERS + 1, nb, owned + 8, cases), F32),
+            pltpu.VMEM((1, cases), F32),
             pltpu.VMEM((1, cases), F32),
         ]
         + [dma((4,))]
@@ -567,8 +567,7 @@
         + [dma((1,))] * 2
         + [dma((4,))] * 2
         + [dma((1,))] * 4
-        + [dma((ITERS,))] * 4
-        + [dma((2 * ITERS,))] * 4
+        + [dma((ITERS + 1,))] * 4
     )
     x, r = pl.pallas_call(
         functools.partial(kernel, sizes),
@@ -592,9 +591,8 @@
     x, r = pl.pallas_call(
         deliver,
         out_shape=(shape, shape),
-        in_specs=[hbm, hbm],
-        out_specs=(hbm, hbm),
-        scratch_shapes=[dma((2,))],
+        in_specs=[vmem, vmem],
+        out_specs=(vmem, vmem),
         name="deliver",
     )(x, r)
     return x[None, None], r[None, None]

time: 201 us -> 168 us (0.84)
  Pallas kernels: 201 us -> 168 us
    pallas_call x1, Pallas kernels: 24.9 us -> 2.02 us  [local(): pl.pallas_call(deliver, out_shape=(shape, shape), in_specs=[vmem, vmem],...]
    pallas_call x1, Pallas kernels: 176 us -> 166 us  [local(): pl.pallas_call(functools.partial(kernel, sizes), out_shape=(shape, shape)...]
where the time goes in v3:
time: 168 us
  Pallas kernels  168 us (100%)
    pallas_call x1, Pallas kernels, local(): pl.pallas_call(functools.partial(kernel, sizes), out_shape=(shape, shape)...  166 us

profile of v3, /device:TPU:1, one launch (start us, length us, event | category | flops | bytes accessed | tf_op | source)
XLA Modules:
  0.0 168.3 jit_solution(7026633732398051538)
XLA Ops:
  0.6 165.6 %bddc_cg.1 = (f32[768,128]{1,0:T(8,128)}, f32[768,128]{1,0:T(8,128)}) custom-call(f32[768,128]{1,0:T(8,128)} %bitcast.12, f32[768,1536]{1,0:T(8,128)} %bitcast.10, f32[768,1536]{1,0:T(8,128)} %bitcast.11, f32[8,768]{1,0:T(8,128)} %bitcast.13, s32[4,192]{1,0:T(4,128)} %bitcast.14, s32[8]{0:T(128)} %bitcast.15, f32[8,2048]{1,0:T(8,128)} %coarse_ref.1), custom_call_target="tpu_custom_call" | custom-call | tf_op jit(solution)/shard_map/bddc_cg/pallas_call | solution.py:572
  166.2 2.0 %deliver.1 = (f32[768,128]{1,0:T(8,128)}, f32[768,128]{1,0:T(8,128)}) custom-call(f32[768,128]{1,0:T(8,128)} %get-tuple-element.6.x_ref, f32[768,128]{1,0:T(8,128)} %get-tuple-element.7.r_ref), custom_call_target="tpu_custom_call" | custom-call | tf_op jit(solution)/shard_map/deliver/pallas_call | solution.py:591

commit v4 on v3

--- a/solution.py
+++ b/solution.py
@@ -45,11 +45,11 @@
     lf, sf, lhi, llo, shi, slo,
     face_tx, face_rx, own, ply_rx,
     pdir, simg, mdir, upre, raw, acc, tb, perm, psc, pst,
-    fwd_tx, pmap, nbr, dpad, wblk, cblk, lists,
+    fwd_tx, pmap, nbr, dpad, wblk, chi, clo, lists, psn_tx, psn_rx, psn, tsm_tx, tsm_rx,
     sums, co1, ytx, co2, rz_ref, pap_ref,
     load_sem, face_ss, face_rs, ply_ss, ply_rs, fwd_ss, map_ss, map_rs,
     nbr_ss, nbr_rs, win_ss, win_rs, list_ss, list_rs,
-    co1_ss, co1_rs, co2_ss, co2_rs,
+    co1_ss, co1_rs, co2_ss, co2_rs, psn_ss, psn_rs, tsm_ss, tsm_rs,
 ):
     nb, nm, npl = sizes
     ng = nm * npl
@@ -81,9 +81,21 @@
     at_end = jnp.logical_or(place == 0, place == run - 1)
     serves_end = jnp.logical_or(place == 1, place == run - 2)
     toward_end = (jnp.where(first == 0, b_prev, b_next), m, p)
+    from_end = (jnp.where(first == 0, b_next, b_prev), m, p)
+
+    def device_at(f):
+        if isinstance(f, int):
+            return neighbour[f]
+        return toward_end if f is first else from_end
+
+    def opposite(f):
+        return f ^ 1 if isinstance(f, int) else 1 - f
+
+    def weight_of(f):
+        return weight[f] if isinstance(f, int) else 0.5
 
     def guarded(f, fn):
-        if exists[f] is None:
+        if not isinstance(f, int) or exists[f] is None:
             fn()
         else:
             pl.when(exists[f])(fn)
@@ -136,6 +148,8 @@
 
             lax.fori_loop(0, EXCH, clear, 0)
             nbr[1 + f] = jnp.zeros(nbr.shape[1:], F32)
+            for it in range(ITERS):
+                tsm_rx[it, f] = jnp.zeros((owned, cases), F32)
 
     map_copy = remote(map_ref, pmap, map_ss.at[0], map_rs.at[0], partner)
 
@@ -152,22 +166,30 @@
         return (out[:, 2 * cases :] + out[:, cases : 2 * cases]) + out[:, :cases]
 
     def face_copy(e, f):
+        there = opposite(f)
         return remote(
-            face_tx.at[e, f], face_rx.at[e, f ^ 1], face_ss.at[e, f], face_rs.at[e, f ^ 1], neighbour[f]
+            face_tx.at[e, f], face_rx.at[e, there], face_ss.at[e, f], face_rs.at[e, there], device_at(f)
         )
 
-    def face_send(e, f, value):
+    def face_send(e, f):
         def go():
-            face_tx[e, f] = permute(f, value)
+            face_tx[e, f] = permute(f, raw[f])
             face_copy(e, f).start()
 
         guarded(f, go)
+
+    def faces_send(e):
+        pl.when(at_end)(lambda: face_send(e, first))
+        face_send(e, 2)
+        face_send(e, 3)
+        pl.when(jnp.logical_not(at_end))(lambda: face_send(e, first))
+        face_send(e, second)
 
     def face_wait(e, f):
         guarded(
             f,
             lambda: remote(
-                face_tx.at[e, f], face_rx.at[e, f], face_ss.at[e, f], face_rs.at[e, f], neighbour[f]
+                face_tx.at[e, f], face_rx.at[e, f], face_ss.at[e, f], face_rs.at[e, f], device_at(f)
             ).wait_recv(),
         )
 
@@ -194,10 +216,6 @@
     def ply_send_mer(e):
         ply_copy(e, 2).start()
         when(jnp.logical_not(has_hi), lambda: ply_copy(e, 3).start())
-
-    def ply_send_cycle(e):
-        ply_copy(e, first).start()
-        when(jnp.logical_not(at_end), lambda: ply_copy(e, second).start())
 
     def pass_mer(e):
         ply_copy(e, 2).wait_recv()
@@ -235,12 +253,9 @@
     def group_second(it, coarse):
         batch(co1, it, ng, co1_ss.at[it], co1_rs.at[it]).wait_recv()
         if coarse:
-            y = jnp.dot(
-                cblk[...],
-                co1[it, :, pl.ds(0, owned)].reshape(ng * owned, cases),
-                precision=HIGH,
-                preferred_element_type=F32,
-            )
+            high, low = halves(co1[it, :, pl.ds(0, owned)].reshape(ng * owned, cases))
+            both = dot(chi[...], jnp.concatenate([high, low], axis=1))
+            y = (both[:, :cases] + both[:, cases:]) + dot(clo[...], high)
             ytx[it, :, pl.ds(0, owned)] = y.reshape(nb, owned, cases)
         else:
             ytx[it, :, pl.ds(0, owned)] = jnp.zeros((nb, owned, cases), F32)
@@ -271,21 +286,71 @@
 
     def store_split(side, f, value):
         hi, lo = halves(value)
-        part = pl.ds(f * face, face)
-        tb[side, part, pl.ds(0, cases)] = hi
-        tb[side, part, pl.ds(cases, cases)] = lo
+        tb[side, f, :, pl.ds(0, cases)] = hi
+        tb[side, f, :, pl.ds(cases, cases)] = lo
 
     def product(hi, lo, side, pair):
         part = pl.ds(2 * pair * face, 2 * face)
-        both = dot(hi[side, :, part], tb[side, part, :])
-        small = dot(lo[side, :, part], tb[side, part, pl.ds(0, cases)])
-        return (both[:, :cases] + both[:, cases:]) + small
+        vector = tb[side, pl.ds(2 * pair, 2)].reshape(2 * face, 2 * cases)
+        both = dot(hi[side, :, part], vector)
+        small = dot(lo[side, :, part], vector[:, :cases])
+        return ((both[:, :cases] + both[:, cases:]) + small).reshape(4, face, cases)
+
+    def terms_copy(it, f):
+        there = opposite(f)
+        return remote(
+            tsm_tx.at[it, f], tsm_rx.at[it, there], tsm_ss.at[it, f], tsm_rs.at[it, there], device_at(f)
+        )
+
+    def three_parts(value):
+        return value[:owned, :cases] + value[:owned, cases:] + value[owned:, :cases]
+
+    def terms_send(it):
+        for f in range(4):
+            store_split(1, f, weight[f] * raw[f])
+        for f in (0, 1, 2, 3):
+
+            def go():
+                tsm_tx[it, f] = three_parts(dot(psn[f], tb[1, f]))
+                terms_copy(it, f).start()
+
+            guarded(f, go)
+        co1[it, mp, pl.ds(0, owned)] = three_parts(dot(pst[...], tb[1].reshape(half, 2 * cases)))
+
+    def terms_end(it):
+        total = co1[it, mp, pl.ds(0, owned)]
+        for f in (2, 3, 0, 1):
+            guarded(
+                f,
+                lambda: remote(
+                    tsm_tx.at[it, f], tsm_rx.at[it, f], tsm_ss.at[it, f], tsm_rs.at[it, f], device_at(f)
+                ).wait_recv(),
+            )
+            total += tsm_rx[it, f]
+        return total
+
+    def terms_sent(it):
+        for f in range(4):
+            guarded(f, lambda f=f: terms_copy(it, f).wait_send())
 
     pl.semaphore_wait(barrier, ng - 1 + nb - 1)
 
-    for f in (2, 3, 0, 1):
-        raw[f] = loads_ref[pl.ds(f * face, face), :]
-        face_send(0, f, raw[f])
+    def psn_copy(f):
+        there = opposite(f)
+        return remote(psn_tx.at[f], psn_rx.at[there], psn_ss.at[f], psn_rs.at[there], device_at(f))
+
+    for f in range(4):
+
+        def go():
+            hi, mid, lo = thirds(psi_ref[:, pl.ds(f * face, face)])
+            stacked = jnp.concatenate(
+                [hi.astype(F32), mid.astype(F32), lo.astype(F32)], axis=0
+            ).astype(BF16)
+            out = lax.dot_general(stacked, perm[f], NT, preferred_element_type=F32)
+            psn_tx[f] = (out[2 * owned :] + out[owned : 2 * owned]) + out[:owned]
+            psn_copy(f).start()
+
+        guarded(f, go)
 
     slot_there = [2, 1, 4, 3]
 
@@ -298,6 +363,10 @@
     map_copy.start()
     nbr[0] = coarse_ref[...]
     spread(mp, mp_devices, lambda _: lists.at[mp], lists.at[mp], list_ss.at[0], list_rs.at[0])
+
+    for f in range(4):
+        raw[f] = loads_ref[pl.ds(f * face, face), :]
+    faces_send(0)
 
     psi_hi, psi_lo = halves(psi_ref[...])
     psi_hi, psi_lo = psi_hi.astype(F32), psi_lo.astype(F32)
@@ -321,9 +390,17 @@
 
         lax.fori_loop(0, half // 64, step, 0)
 
-    fetches[0].wait()
-    fetches[1].wait()
-    split_matrix(lf, lhi, llo)
+    for f in range(4):
+
+        def go():
+            remote(
+                psn_tx.at[f], psn_rx.at[f], psn_ss.at[f], psn_rs.at[f], device_at(f)
+            ).wait_recv()
+            hi, lo = halves(psn_rx[f])
+            psn[f] = jnp.concatenate([hi.astype(F32), lo.astype(F32)], axis=0).astype(BF16)
+
+        guarded(f, go)
+    terms_send(0)
 
     group = ng * owned
     this = (b * nm + m) * npl + p
@@ -350,15 +427,18 @@
                 coarse_ref, nbr.at[1 + f], nbr_ss.at[f], nbr_rs.at[f], neighbour[f]
             ).wait_recv(),
         )
-    named = jnp.dot(
-        selector, nbr[...].reshape(5 * owned, nbr.shape[2]), precision=HIGH, preferred_element_type=F32
-    )
+    hot = selector.astype(BF16)
+    hi, mid, lo = thirds(nbr[...].reshape(5 * owned, nbr.shape[2]))
+    named = (dot(hot, lo) + dot(hot, mid)) + dot(hot, hi)
     for j in range(nb + 2):
         block = (j - 1) % nb
         dpad[j] = named[:, block * group : (block + 1) * group]
     wblk[b] = dpad[pl.ds(b, 3)]
     spread(b, blk_devices, lambda peer: dpad.at[pl.ds(peer, 3)], wblk.at[b], win_ss.at[0], win_rs.at[0])
 
+    fetches[0].wait()
+    fetches[1].wait()
+    split_matrix(lf, lhi, llo)
     map_copy.wait_recv()
     for f in range(3):
         perm[4 + f] = jnp.where(rows == pmap[f : f + 1, :], 1.0, 0.0).astype(BF16)
@@ -375,10 +455,15 @@
         remote(block, block, win_ss.at[0], win_rs.at[0], partner).wait_recv()
         total = jnp.zeros((nb * owned, group), F32)
         for j, start in enumerate((b_prev, b, b_next)):
-            hot = jnp.where(names == column + start * group, 1.0, 0.0).astype(F32)
+            hot = jnp.where(names == column + start * group, 1.0, 0.0).astype(BF16)
             window = wblk[:, j].reshape(nb * owned, group)
-            total += lax.dot_general(window, hot, NT, precision=HIGH, preferred_element_type=F32)
-        cblk[...] = total
+            hi, mid, lo = (
+                lax.dot_general(piece, hot, NT, preferred_element_type=F32) for piece in thirds(window)
+            )
+            total += (lo + mid) + hi
+        chi[...], clo[...] = halves(total)
+        for f in range(4):
+            guarded(f, lambda f=f: psn_copy(f).wait_send())
         for f in range(4):
             guarded(f, lambda f=f: nbr_copy(f).wait_send())
         block = lists.at[pl.ds(0, ng - 1)]
@@ -387,37 +472,52 @@
         remote(block, block, win_ss.at[0], win_rs.at[0], partner).wait_send()
         map_copy.wait_send()
 
-    def assemble(e, pair, weights, ply):
-        for f in (2 * pair, 2 * pair + 1):
-            face_wait(e, f)
-            value = raw[f] + face_rx[e, f]
-            own[e, f] = value
-        if ply and pair:
-            ply_send_mer(e)
-        elif ply:
-            ply_send_cycle(e)
-        if ply:
-            for f in (2 * pair, 2 * pair + 1):
-                value = own[e, f]
-                store_split(0, f, value if weights is None else weights[f] * value)
-
-    def exchange(e, hi, lo, weights, begin, middle):
-        assemble(e, 1, weights, True)
+    def assemble(e, f):
+        face_wait(e, f)
+        own[e, f] = raw[f] + face_rx[e, f]
+
+    def exchange(e, hi, lo, weights, early, middle):
+        def scaled(f, value):
+            return value if weights is None else weight_of(f) * value
+
+        def take(f):
+            assemble(e, f)
+            store_split(0, f, scaled(f, own[e, f]))
+
+        def add(side, pair):
+            acc[...] += product(hi, lo, side, pair)
+
+        take(2)
+        take(3)
+        ply_send_mer(e)
+        early()
         acc[...] = product(hi, lo, 0, 1)
-        assemble(e, 0, weights, True)
-        begin()
+        take(second)
+
+        @pl.when(jnp.logical_not(at_end))
+        def _():
+            take(first)
+            ply_copy(e, first).start()
+            ply_copy(e, second).start()
+            add(0, 0)
+
         pass_mer(e)
-        acc[...] += product(hi, lo, 0, 0)
+        middle()
+
+        @pl.when(at_end)
+        def _():
+            take(first)
+            ply_copy(e, first).start()
+            add(0, 0)
+
         pass_end(e)
-        middle()
         ply_copy(e, 3).wait_recv()
         for pair in (1, 0):
             if pair == 0:
                 ply_copy(e, second).wait_recv()
             for f in (2 * pair, 2 * pair + 1):
-                value = ply_rx[e, f]
-                store_split(1, f, value if weights is None else weights[f] * value)
-            acc[...] += product(hi, lo, 1, pair)
+                store_split(1, f, scaled(f, ply_rx[e, f]))
+            add(1, pair)
 
     def steps(it, rz, energy, cross):
         beta = jnp.where(it <= 1, 0.0, rz / rz_ref[...])
@@ -449,9 +549,8 @@
         e1 = 2 * it
         e2 = e1 + 1
 
-        def begin():
-            parts = dot(pst[...], tb[0])
-            group_first(it, parts[:owned, :cases] + parts[:owned, cases:] + parts[owned:, :cases])
+        def early():
+            group_first(it, terms_end(it))
 
         def middle():
             @pl.when(it == 0)
@@ -466,20 +565,19 @@
                 fetches[3].wait()
                 split_matrix(sf, shi, slo)
 
-        exchange(e1, lhi, llo, weight, begin, middle)
+        exchange(e1, lhi, llo, weight, early, middle)
         picked, rz, energy, cross = group_end(it)
         pick_hi = picked.astype(BF16).astype(F32)
         stack = jnp.concatenate([pick_hi, picked - pick_hi, pick_hi], axis=0).astype(BF16)
-        acc[...] += dot(psc[...], stack)
+        correction = dot(psc[...], stack).reshape(4, face, cases)
         alpha, beta = steps(it, rz, energy, cross)
-        for f in (2, 3, 0, 1):
-            change = acc[pl.ds(f * face, face), :] + beta * mdir[f]
+        for f in range(4):
+            change = (acc[f] + correction[f]) + beta * mdir[f]
             mdir[f] = change
             value = upre[f] - alpha * change
             upre[f] = value
-            value = weight[f] * value
-            raw[f] = value
-            face_send(e2, f, value)
+            raw[f] = weight[f] * value
+        faces_send(e2)
         advance(e1, alpha, beta)
         partial = jnp.zeros((8, cases), F32)
         for f in range(4):
@@ -487,12 +585,12 @@
         faces_sent(e1)
         ply_sent(e1)
         group_sent(it)
+        terms_sent(it)
 
         exchange(e2, shi, slo, None, lambda: None, lambda: None)
-        for f in (2, 3, 0, 1):
-            value = acc[pl.ds(f * face, face), :]
-            raw[f] = value
-            face_send(e2 + 1, f, value)
+        raw[...] = acc[...]
+        pl.when(it + 1 < ITERS)(lambda: terms_send(it + 1))
+        faces_send(e2 + 1)
         energy = jnp.zeros((8, cases), F32)
         cross = jnp.zeros((8, cases), F32)
         for f in range(4):
@@ -507,9 +605,11 @@
 
     last = EXCH - 1
     group_first(ITERS, jnp.zeros((owned, cases), F32))
-    assemble(last, 1, None, False)
+    assemble(last, 2)
+    assemble(last, 3)
     group_second(ITERS, False)
-    assemble(last, 0, None, False)
+    assemble(last, 0)
+    assemble(last, 1)
     _, rz, energy, cross = group_end(ITERS)
     alpha, beta = steps(ITERS, rz, energy, cross)
     advance(last, alpha, beta)
@@ -541,8 +641,8 @@
         + [pltpu.VMEM((EXCH,) + faces, F32)] * 4
         + [pltpu.VMEM(faces, F32)] * 5
         + [
-            pltpu.VMEM((half, cases), F32),
-            pltpu.VMEM((2, half, 2 * cases), BF16),
+            pltpu.VMEM(faces, F32),
+            pltpu.VMEM((2, 4, face, 2 * cases), BF16),
             pltpu.VMEM((7, face, face), BF16),
             pltpu.VMEM((half, 3 * owned), BF16),
             pltpu.VMEM((2 * owned, half), BF16),
@@ -551,8 +651,14 @@
             pltpu.VMEM((5, owned, coarse), F32),
             pltpu.VMEM((nb + 2, owned, group), F32),
             pltpu.VMEM((nb, 3, owned, group), F32),
-            pltpu.VMEM((nb * owned, group), F32),
+            pltpu.VMEM((nb * owned, group), BF16),
+            pltpu.VMEM((nb * owned, group), BF16),
             pltpu.VMEM((ng, owned, 128), jnp.int32),
+            pltpu.VMEM((4, owned, face), F32),
+            pltpu.VMEM((4, owned, face), F32),
+            pltpu.VMEM((4, 2 * owned, face), BF16),
+            pltpu.VMEM((ITERS, 4, owned, cases), F32),
+            pltpu.VMEM((ITERS, 4, owned, cases), F32),
             pltpu.VMEM((8, cases), F32),
             pltpu.VMEM((ITERS + 1, ng, owned + 8, cases), F32),
             pltpu.VMEM((ITERS + 1, nb, owned + 8, cases), F32),
@@ -568,6 +674,8 @@
         + [dma((4,))] * 2
         + [dma((1,))] * 4
         + [dma((ITERS + 1,))] * 4
+        + [dma((4,))] * 2
+        + [dma((ITERS, 4))] * 2
     )
     x, r = pl.pallas_call(
         functools.partial(kernel, sizes),

time: 168 us -> 156 us (0.929)
  Pallas kernels: 168 us -> 155 us
    pallas_call x1, Pallas kernels: 166 us -> 153 us  [local(): pl.pallas_call(functools.partial(kernel, sizes), out_shape=(shape, shape)...]
where the time goes in v4:
time: 156 us
  Pallas kernels  155 us (99%)
    pallas_call x1, Pallas kernels, local(): pl.pallas_call(functools.partial(kernel, sizes), out_shape=(shape, shape)...  153 us

profile of v4, /device:TPU:1, one launch (start us, length us, event | category | flops | bytes accessed | tf_op | source)
XLA Modules:
  0.0 155.8 jit_solution(15675077038412594689)
XLA Ops:
  0.6 153.1 %bddc_cg.1 = (f32[768,128]{1,0:T(8,128)}, f32[768,128]{1,0:T(8,128)}) custom-call(f32[768,128]{1,0:T(8,128)} %bitcast.12, f32[768,1536]{1,0:T(8,128)} %bitcast.10, f32[768,1536]{1,0:T(8,128)} %bitcast.11, f32[8,768]{1,0:T(8,128)} %bitcast.13, s32[4,192]{1,0:T(4,128)} %bitcast.14, s32[8]{0:T(128)} %bitcast.15, f32[8,2048]{1,0:T(8,128)} %coarse_ref.1), custom_call_target="tpu_custom_call" | custom-call | tf_op jit(solution)/shard_map/bddc_cg/pallas_call | solution.py:680
  153.8 2.0 %deliver.1 = (f32[768,128]{1,0:T(8,128)}, f32[768,128]{1,0:T(8,128)}) custom-call(f32[768,128]{1,0:T(8,128)} %get-tuple-element.6.x_ref, f32[768,128]{1,0:T(8,128)} %get-tuple-element.7.r_ref), custom_call_target="tpu_custom_call" | custom-call | tf_op jit(solution)/shard_map/deliver/pallas_call | solution.py:699

commit v5 on v4

--- a/solution.py
+++ b/solution.py
@@ -79,7 +79,6 @@
     first = jnp.where(place < run // 2, 0, 1)
     second = 1 - first
     at_end = jnp.logical_or(place == 0, place == run - 1)
-    serves_end = jnp.logical_or(place == 1, place == run - 2)
     toward_end = (jnp.where(first == 0, b_prev, b_next), m, p)
     from_end = (jnp.where(first == 0, b_next, b_prev), m, p)
 
@@ -202,44 +201,25 @@
 
     def mer_forward(e):
         return remote(
-            fwd_tx.at[e, 0], ply_rx.at[e, 3], fwd_ss.at[e, 0], ply_rs.at[e, 3], neighbour[2]
-        )
-
-    def end_forward(e):
-        return remote(
-            fwd_tx.at[e, 1], ply_rx.at[e, second], fwd_ss.at[e, 1], ply_rs.at[e, second], toward_end
+            fwd_tx.at[e], ply_rx.at[e, 3], fwd_ss.at[e], ply_rs.at[e, 3], neighbour[2]
         )
 
     def when(condition, fn):
         pl.when(condition)(fn)
 
-    def ply_send_mer(e):
-        ply_copy(e, 2).start()
-        when(jnp.logical_not(has_hi), lambda: ply_copy(e, 3).start())
-
     def pass_mer(e):
         ply_copy(e, 2).wait_recv()
 
         @pl.when(has_lo)
         def _():
-            fwd_tx[e, 0] = permute(6, ply_rx[e, 2])
+            fwd_tx[e] = permute(4, ply_rx[e, 2])
             mer_forward(e).start()
 
-    def pass_end(e):
-        ply_copy(e, first).wait_recv()
-
-        @pl.when(serves_end)
-        def _():
-            fwd_tx[e, 1] = permute(4 + first, ply_rx[e, first])
-            end_forward(e).start()
-
     def ply_sent(e):
-        ply_copy(e, 2).wait_send()
+        for f in (0, 1, 2):
+            ply_copy(e, f).wait_send()
         when(jnp.logical_not(has_hi), lambda: ply_copy(e, 3).wait_send())
-        ply_copy(e, first).wait_send()
-        when(jnp.logical_not(at_end), lambda: ply_copy(e, second).wait_send())
         when(has_lo, lambda: mer_forward(e).wait_send())
-        when(serves_end, lambda: end_forward(e).wait_send())
 
     def batch(buffer, index, count, send, recv):
         block = buffer.at[index, pl.ds(0, count - 1)]
@@ -333,41 +313,6 @@
         for f in range(4):
             guarded(f, lambda f=f: terms_copy(it, f).wait_send())
 
-    pl.semaphore_wait(barrier, ng - 1 + nb - 1)
-
-    def psn_copy(f):
-        there = opposite(f)
-        return remote(psn_tx.at[f], psn_rx.at[there], psn_ss.at[f], psn_rs.at[there], device_at(f))
-
-    for f in range(4):
-
-        def go():
-            hi, mid, lo = thirds(psi_ref[:, pl.ds(f * face, face)])
-            stacked = jnp.concatenate(
-                [hi.astype(F32), mid.astype(F32), lo.astype(F32)], axis=0
-            ).astype(BF16)
-            out = lax.dot_general(stacked, perm[f], NT, preferred_element_type=F32)
-            psn_tx[f] = (out[2 * owned :] + out[owned : 2 * owned]) + out[:owned]
-            psn_copy(f).start()
-
-        guarded(f, go)
-
-    slot_there = [2, 1, 4, 3]
-
-    def nbr_copy(f):
-        slot = slot_there[f]
-        return remote(coarse_ref, nbr.at[slot], nbr_ss.at[f], nbr_rs.at[slot - 1], neighbour[f])
-
-    for f in range(4):
-        guarded(f, lambda f=f: nbr_copy(f).start())
-    map_copy.start()
-    nbr[0] = coarse_ref[...]
-    spread(mp, mp_devices, lambda _: lists.at[mp], lists.at[mp], list_ss.at[0], list_rs.at[0])
-
-    for f in range(4):
-        raw[f] = loads_ref[pl.ds(f * face, face), :]
-    faces_send(0)
-
     psi_hi, psi_lo = halves(psi_ref[...])
     psi_hi, psi_lo = psi_hi.astype(F32), psi_lo.astype(F32)
     pst[...] = jnp.concatenate([psi_hi, psi_lo], axis=0).astype(BF16)
@@ -389,18 +334,6 @@
             return carry
 
         lax.fori_loop(0, half // 64, step, 0)
-
-    for f in range(4):
-
-        def go():
-            remote(
-                psn_tx.at[f], psn_rx.at[f], psn_ss.at[f], psn_rs.at[f], device_at(f)
-            ).wait_recv()
-            hi, lo = halves(psn_rx[f])
-            psn[f] = jnp.concatenate([hi.astype(F32), lo.astype(F32)], axis=0).astype(BF16)
-
-        guarded(f, go)
-    terms_send(0)
 
     group = ng * owned
     this = (b * nm + m) * npl + p
@@ -420,6 +353,41 @@
     for k in range(owned):
         slots = jnp.where(tall == k, list_ref[k], slots)
     selector = jnp.where(slots == names, 1.0, 0.0).astype(F32)
+    pl.semaphore_wait(barrier, ng - 1 + nb - 1)
+
+    slot_there = [2, 1, 4, 3]
+
+    def nbr_copy(f):
+        slot = slot_there[f]
+        return remote(coarse_ref, nbr.at[slot], nbr_ss.at[f], nbr_rs.at[slot - 1], neighbour[f])
+
+    for f in range(4):
+        guarded(f, lambda f=f: nbr_copy(f).start())
+    map_copy.start()
+    nbr[0] = coarse_ref[...]
+    spread(mp, mp_devices, lambda _: lists.at[mp], lists.at[mp], list_ss.at[0], list_rs.at[0])
+
+    def psn_copy(f):
+        there = opposite(f)
+        return remote(psn_tx.at[f], psn_rx.at[there], psn_ss.at[f], psn_rs.at[there], device_at(f))
+
+    for f in range(4):
+
+        def go():
+            hi, mid, lo = thirds(psi_ref[:, pl.ds(f * face, face)])
+            stacked = jnp.concatenate(
+                [hi.astype(F32), mid.astype(F32), lo.astype(F32)], axis=0
+            ).astype(BF16)
+            out = lax.dot_general(stacked, perm[f], NT, preferred_element_type=F32)
+            psn_tx[f] = (out[2 * owned :] + out[owned : 2 * owned]) + out[:owned]
+            psn_copy(f).start()
+
+        guarded(f, go)
+
+    for f in range(4):
+        raw[f] = loads_ref[pl.ds(f * face, face), :]
+    faces_send(0)
+
     for f in range(4):
         guarded(
             f,
@@ -436,12 +404,23 @@
     wblk[b] = dpad[pl.ds(b, 3)]
     spread(b, blk_devices, lambda peer: dpad.at[pl.ds(peer, 3)], wblk.at[b], win_ss.at[0], win_rs.at[0])
 
+    for f in range(4):
+
+        def go():
+            remote(
+                psn_tx.at[f], psn_rx.at[f], psn_ss.at[f], psn_rs.at[f], device_at(f)
+            ).wait_recv()
+            hi, lo = halves(psn_rx[f])
+            psn[f] = jnp.concatenate([hi.astype(F32), lo.astype(F32)], axis=0).astype(BF16)
+
+        guarded(f, go)
+    terms_send(0)
+
     fetches[0].wait()
     fetches[1].wait()
     split_matrix(lf, lhi, llo)
     map_copy.wait_recv()
-    for f in range(3):
-        perm[4 + f] = jnp.where(rows == pmap[f : f + 1, :], 1.0, 0.0).astype(BF16)
+    perm[4] = jnp.where(rows == pmap[2:3, :], 1.0, 0.0).astype(BF16)
     for state in (x_ref, r_ref, pdir, simg, mdir, upre, pap_ref, sums):
         state[...] = jnp.zeros_like(state)
     rz_ref[...] = jnp.ones_like(rz_ref)
@@ -480,41 +459,55 @@
         def scaled(f, value):
             return value if weights is None else weight_of(f) * value
 
-        def take(f):
-            assemble(e, f)
-            store_split(0, f, scaled(f, own[e, f]))
-
         def add(side, pair):
             acc[...] += product(hi, lo, side, pair)
 
-        take(2)
-        take(3)
-        ply_send_mer(e)
+        def pair_send(one, two):
+            assemble(e, one)
+            ply_copy(e, one).start()
+            assemble(e, two)
+            if isinstance(two, int):
+                when(jnp.logical_not(has_hi), lambda: ply_copy(e, 3).start())
+            else:
+                ply_copy(e, two).start()
+
+        def split(f):
+            store_split(0, f, scaled(f, own[e, f]))
+
+        pair_send(2, 3)
         early()
+        split(2)
+        split(3)
         acc[...] = product(hi, lo, 0, 1)
-        take(second)
 
         @pl.when(jnp.logical_not(at_end))
         def _():
-            take(first)
-            ply_copy(e, first).start()
+            pair_send(first, second)
+            split(0)
+            split(1)
+            add(0, 0)
+
+        @pl.when(at_end)
+        def _():
+            assemble(e, second)
             ply_copy(e, second).start()
-            add(0, 0)
+            split(second)
 
         pass_mer(e)
         middle()
 
         @pl.when(at_end)
         def _():
-            take(first)
+            assemble(e, first)
             ply_copy(e, first).start()
+            split(first)
             add(0, 0)
 
-        pass_end(e)
         ply_copy(e, 3).wait_recv()
         for pair in (1, 0):
             if pair == 0:
                 ply_copy(e, second).wait_recv()
+                ply_copy(e, first).wait_recv()
             for f in (2 * pair, 2 * pair + 1):
                 store_split(1, f, scaled(f, ply_rx[e, f]))
             add(1, pair)
@@ -643,10 +636,10 @@
         + [
             pltpu.VMEM(faces, F32),
             pltpu.VMEM((2, 4, face, 2 * cases), BF16),
-            pltpu.VMEM((7, face, face), BF16),
+            pltpu.VMEM((5, face, face), BF16),
             pltpu.VMEM((half, 3 * owned), BF16),
             pltpu.VMEM((2 * owned, half), BF16),
-            pltpu.VMEM((EXCH, 2, face, cases), F32),
+            pltpu.VMEM((EXCH, face, cases), F32),
             pltpu.VMEM((4, face), jnp.int32),
             pltpu.VMEM((5, owned, coarse), F32),
             pltpu.VMEM((nb + 2, owned, group), F32),
@@ -669,7 +662,7 @@
         + [dma((4,))]
         + [dma((EXCH, 4))] * 2
         + [dma((EXCH, 4))] * 2
-        + [dma((EXCH, 2))]
+        + [dma((EXCH,))]
         + [dma((1,))] * 2
         + [dma((4,))] * 2
         + [dma((1,))] * 4

time: 156 us -> 155 us (level)
  no operation moved by 1% of the time
where the time goes in v5:
time: 155 us
  Pallas kernels  154 us (99%)
    pallas_call x1, Pallas kernels, local(): pl.pallas_call(functools.partial(kernel, sizes), out_shape=(shape, shape)...  152 us

profile of v5, /device:TPU:1, one launch (start us, length us, event | category | flops | bytes accessed | tf_op | source)
XLA Modules:
  0.0 154.6 jit_solution(8311774026328862128)
XLA Ops:
  0.6 151.9 %bddc_cg.1 = (f32[768,128]{1,0:T(8,128)}, f32[768,128]{1,0:T(8,128)}) custom-call(f32[768,128]{1,0:T(8,128)} %bitcast.12, f32[768,1536]{1,0:T(8,128)} %bitcast.10, f32[768,1536]{1,0:T(8,128)} %bitcast.11, f32[8,768]{1,0:T(8,128)} %bitcast.13, s32[4,192]{1,0:T(4,128)} %bitcast.14, s32[8]{0:T(128)} %bitcast.15, f32[8,2048]{1,0:T(8,128)} %coarse_ref.1), custom_call_target="tpu_custom_call" | custom-call | tf_op jit(solution)/shard_map/bddc_cg/pallas_call | solution.py:673
  152.6 2.0 %deliver.1 = (f32[768,128]{1,0:T(8,128)}, f32[768,128]{1,0:T(8,128)}) custom-call(f32[768,128]{1,0:T(8,128)} %get-tuple-element.6.x_ref, f32[768,128]{1,0:T(8,128)} %get-tuple-element.7.r_ref), custom_call_target="tpu_custom_call" | custom-call | tf_op jit(solution)/shard_map/deliver/pallas_call | solution.py:692

commit v6 on v5

--- a/solution.py
+++ b/solution.py
@@ -45,11 +45,11 @@
     lf, sf, lhi, llo, shi, slo,
     face_tx, face_rx, own, ply_rx,
     pdir, simg, mdir, upre, raw, acc, tb, perm, psc, pst,
-    fwd_tx, pmap, nbr, dpad, wblk, chi, clo, lists, psn_tx, psn_rx, psn, tsm_tx, tsm_rx,
+    fwd_tx, far_tx, far_rx, pmap, nbr, dpad, wblk, chi, clo, lists, psn_tx, psn_rx, psn, tsm_tx, tsm_rx,
     sums, co1, ytx, co2, rz_ref, pap_ref,
     load_sem, face_ss, face_rs, ply_ss, ply_rs, fwd_ss, map_ss, map_rs,
     nbr_ss, nbr_rs, win_ss, win_rs, list_ss, list_rs,
-    co1_ss, co1_rs, co2_ss, co2_rs, psn_ss, psn_rs, tsm_ss, tsm_rs,
+    co1_ss, co1_rs, co2_ss, co2_rs, psn_ss, psn_rs, tsm_ss, tsm_rs, far_ss, far_rs,
 ):
     nb, nm, npl = sizes
     ng = nm * npl
@@ -81,6 +81,7 @@
     at_end = jnp.logical_or(place == 0, place == run - 1)
     toward_end = (jnp.where(first == 0, b_prev, b_next), m, p)
     from_end = (jnp.where(first == 0, b_next, b_prev), m, p)
+    across_end = (jnp.where(first == 0, b_prev, b_next), m, q)
 
     def device_at(f):
         if isinstance(f, int):
@@ -133,6 +134,10 @@
     greet(mp, mp_devices)
     greet(b, blk_devices)
 
+    @pl.when(at_end)
+    def _():
+        pl.semaphore_signal(barrier, inc=1, device_id=across_end, device_id_type=MESH)
+
     rows = lax.broadcasted_iota(jnp.int32, (face, face), 0)
     for f in range(4):
         perm[f] = jnp.where(rows == map_ref[f : f + 1, :], 1.0, 0.0).astype(BF16)
@@ -177,8 +182,23 @@
 
         guarded(f, go)
 
+    def across_copy(e):
+        return remote(face_tx.at[e, first], far_rx.at[e], far_ss.at[e], far_rs.at[e], across_end)
+
+    def far_copy(e):
+        return remote(far_tx.at[e], ply_rx.at[e, first], ply_ss.at[e, first], ply_rs.at[e, first], partner)
+
     def faces_send(e):
-        pl.when(at_end)(lambda: face_send(e, first))
+        @pl.when(at_end)
+        def _():
+            face_send(e, first)
+
+            @pl.when(e < EXCH - 1)
+            def _():
+                across_copy(e).start()
+                far_tx[e] = raw[first]
+                far_copy(e).start()
+
         face_send(e, 2)
         face_send(e, 3)
         pl.when(jnp.logical_not(at_end))(lambda: face_send(e, first))
@@ -216,8 +236,15 @@
             mer_forward(e).start()
 
     def ply_sent(e):
-        for f in (0, 1, 2):
-            ply_copy(e, f).wait_send()
+        ply_copy(e, second).wait_send()
+        ply_copy(e, 2).wait_send()
+        when(jnp.logical_not(at_end), lambda: ply_copy(e, first).wait_send())
+
+        @pl.when(at_end)
+        def _():
+            far_copy(e).wait_send()
+            across_copy(e).wait_send()
+
         when(jnp.logical_not(has_hi), lambda: ply_copy(e, 3).wait_send())
         when(has_lo, lambda: mer_forward(e).wait_send())
 
@@ -353,7 +380,7 @@
     for k in range(owned):
         slots = jnp.where(tall == k, list_ref[k], slots)
     selector = jnp.where(slots == names, 1.0, 0.0).astype(F32)
-    pl.semaphore_wait(barrier, ng - 1 + nb - 1)
+    pl.semaphore_wait(barrier, ng - 1 + nb - 1 + jnp.where(at_end, 1, 0))
 
     slot_there = [2, 1, 4, 3]
 
@@ -499,7 +526,6 @@
         @pl.when(at_end)
         def _():
             assemble(e, first)
-            ply_copy(e, first).start()
             split(first)
             add(0, 0)
 
@@ -508,6 +534,12 @@
             if pair == 0:
                 ply_copy(e, second).wait_recv()
                 ply_copy(e, first).wait_recv()
+
+                @pl.when(at_end)
+                def _():
+                    across_copy(e).wait_recv()
+                    ply_rx[e, first] += far_rx[e]
+
             for f in (2 * pair, 2 * pair + 1):
                 store_split(1, f, scaled(f, ply_rx[e, f]))
             add(1, pair)
@@ -639,6 +671,8 @@
             pltpu.VMEM((5, face, face), BF16),
             pltpu.VMEM((half, 3 * owned), BF16),
             pltpu.VMEM((2 * owned, half), BF16),
+            pltpu.VMEM((EXCH, face, cases), F32),
+            pltpu.VMEM((EXCH, face, cases), F32),
             pltpu.VMEM((EXCH, face, cases), F32),
             pltpu.VMEM((4, face), jnp.int32),
             pltpu.VMEM((5, owned, coarse), F32),
@@ -669,6 +703,7 @@
         + [dma((ITERS + 1,))] * 4
         + [dma((4,))] * 2
         + [dma((ITERS, 4))] * 2
+        + [dma((EXCH,))] * 2
     )
     x, r = pl.pallas_call(
         functools.partial(kernel, sizes),

time: 155 us -> 155 us (level)
  no operation moved by 1% of the time
where the time goes in v6:
time: 155 us
  Pallas kernels  155 us (100%)
    pallas_call x1, Pallas kernels, local(): pl.pallas_call(functools.partial(kernel, sizes), out_shape=(shape, shape)...  153 us

profile of v6, /device:TPU:1, one launch (start us, length us, event | category | flops | bytes accessed | tf_op | source)
XLA Modules:
  0.0 155.3 jit_solution(7911859395918888290)
XLA Ops:
  0.6 152.7 %bddc_cg.1 = (f32[768,128]{1,0:T(8,128)}, f32[768,128]{1,0:T(8,128)}) custom-call(f32[768,128]{1,0:T(8,128)} %bitcast.12, f32[768,1536]{1,0:T(8,128)} %bitcast.10, f32[768,1536]{1,0:T(8,128)} %bitcast.11, f32[8,768]{1,0:T(8,128)} %bitcast.13, s32[4,192]{1,0:T(4,128)} %bitcast.14, s32[8]{0:T(128)} %bitcast.15, f32[8,2048]{1,0:T(8,128)} %coarse_ref.1), custom_call_target="tpu_custom_call" | custom-call | tf_op jit(solution)/shard_map/bddc_cg/pallas_call | solution.py:708
  153.3 2.0 %deliver.1 = (f32[768,128]{1,0:T(8,128)}, f32[768,128]{1,0:T(8,128)}) custom-call(f32[768,128]{1,0:T(8,128)} %get-tuple-element.6.x_ref, f32[768,128]{1,0:T(8,128)} %get-tuple-element.7.r_ref), custom_call_target="tpu_custom_call" | custom-call | tf_op jit(solution)/shard_map/deliver/pallas_call | solution.py:727

commit v7 on v6

--- a/solution.py
+++ b/solution.py
@@ -501,8 +501,8 @@
         def split(f):
             store_split(0, f, scaled(f, own[e, f]))
 
+        early()
         pair_send(2, 3)
-        early()
         split(2)
         split(3)
         acc[...] = product(hi, lo, 0, 1)
@@ -512,7 +512,6 @@
             pair_send(first, second)
             split(0)
             split(1)
-            add(0, 0)
 
         @pl.when(at_end)
         def _():
@@ -520,15 +519,15 @@
             ply_copy(e, second).start()
             split(second)
 
+        middle()
         pass_mer(e)
-        middle()
 
         @pl.when(at_end)
         def _():
             assemble(e, first)
             split(first)
-            add(0, 0)
-
+
+        add(0, 0)
         ply_copy(e, 3).wait_recv()
         for pair in (1, 0):
             if pair == 0:

time: 155 us -> 152 us (0.981)
  Pallas kernels: 155 us -> 151 us
    pallas_call x1, Pallas kernels: 153 us -> 149 us  [local(): pl.pallas_call(functools.partial(kernel, sizes), out_shape=(shape, shape)...]
where the time goes in v7:
time: 152 us
  Pallas kernels  151 us (99%)
    pallas_call x1, Pallas kernels, local(): pl.pallas_call(functools.partial(kernel, sizes), out_shape=(shape, shape)...  149 us

profile of v7, /device:TPU:1, one launch (start us, length us, event | category | flops | bytes accessed | tf_op | source)
XLA Modules:
  0.0 152.1 jit_solution(9333656918111939865)
XLA Ops:
  0.6 149.4 %bddc_cg.1 = (f32[768,128]{1,0:T(8,128)}, f32[768,128]{1,0:T(8,128)}) custom-call(f32[768,128]{1,0:T(8,128)} %bitcast.12, f32[768,1536]{1,0:T(8,128)} %bitcast.10, f32[768,1536]{1,0:T(8,128)} %bitcast.11, f32[8,768]{1,0:T(8,128)} %bitcast.13, s32[4,192]{1,0:T(4,128)} %bitcast.14, s32[8]{0:T(128)} %bitcast.15, f32[8,2048]{1,0:T(8,128)} %coarse_ref.1), custom_call_target="tpu_custom_call" | custom-call | tf_op jit(solution)/shard_map/bddc_cg/pallas_call | solution.py:707
  150.1 2.0 %deliver.1 = (f32[768,128]{1,0:T(8,128)}, f32[768,128]{1,0:T(8,128)}) custom-call(f32[768,128]{1,0:T(8,128)} %get-tuple-element.6.x_ref, f32[768,128]{1,0:T(8,128)} %get-tuple-element.7.r_ref), custom_call_target="tpu_custom_call" | custom-call | tf_op jit(solution)/shard_map/deliver/pallas_call | solution.py:726
